TPU v7x, 32 devices: a whole 2x2x4 slice. The times are simulated.
32 devices in a mesh: fsdp: 8 (over z, x), rep: 4 (over y, core).
Axes of the slice: x: 2, y: 2, z: 4, core: 2. Of those that a mesh axis runs over, the one named last changes fastest.
Arguments:
- patches: bfloat16 [37632, 768], P(('fsdp', 'rep')), may hold values from -6 to 6
- slot_clip: int32 [768], P(('fsdp', 'rep')), may hold values from -1 to 767, as said below
- out_grad: bfloat16 [37632, 768], P(('fsdp', 'rep')), may hold values from -6 to 6
- project_in_weight: float32 [768, 2304], P('fsdp'), may hold values from -0.21875 to 0.21875
- project_in_moment: float32 [768, 2304], P('fsdp'), may hold values from -320 to 320
- project_in_average: float32 [768, 2304], P('fsdp'), may hold values from -0.21875 to 0.21875
- project_out_weight: float32 [768, 768], P('fsdp'), may hold values from -0.625 to 0.625
- project_out_moment: float32 [768, 768], P('fsdp'), may hold values from -320 to 320
- project_out_average: float32 [768, 768], P('fsdp'), may hold values from -0.625 to 0.625
- expand_weight: float32 [768, 3072], P('fsdp'), may hold values from -0.21875 to 0.21875
- expand_moment: float32 [768, 3072], P('fsdp'), may hold values from -320 to 320
- expand_average: float32 [768, 3072], P('fsdp'), may hold values from -0.21875 to 0.21875
- contract_weight: float32 [3072, 768], P('fsdp'), may hold values from -0.109375 to 0.109375
- contract_moment: float32 [3072, 768], P('fsdp'), may hold values from -320 to 320
- contract_average: float32 [3072, 768], P('fsdp'), may hold values from -0.109375 to 0.109375
- vector_weight: float32 [10, 768], P(None, 'fsdp'), may hold values from -1.2 to 1.6, as said below
- vector_moment: float32 [10, 768], P(None, 'fsdp'), may hold values from -512 to 512
- vector_average: float32 [10, 768], P(None, 'fsdp'), may hold values from -1.2 to 1.6, as said below
Outputs:
- block_out: bfloat16 [37632, 768], P(('fsdp', 'rep'))
- patch_grad: float32 [37632, 768], P(('fsdp', 'rep'))
- project_in_grad: float32 [768, 2304], P('fsdp')
- project_in_moment_new: float32 [768, 2304], P('fsdp')
- project_in_weight_new: float32 [768, 2304], P('fsdp')
- project_in_average_new: float32 [768, 2304], P('fsdp')
- project_in_weight_low: bfloat16 [768, 2304], P('fsdp')
- project_out_grad: float32 [768, 768], P('fsdp')
- project_out_moment_new: float32 [768, 768], P('fsdp')
- project_out_weight_new: float32 [768, 768], P('fsdp')
- project_out_average_new: float32 [768, 768], P('fsdp')
- project_out_weight_low: bfloat16 [768, 768], P('fsdp')
- expand_grad: float32 [768, 3072], P('fsdp')
- expand_moment_new: float32 [768, 3072], P('fsdp')
- expand_weight_new: float32 [768, 3072], P('fsdp')
- expand_average_new: float32 [768, 3072], P('fsdp')
- expand_weight_low: bfloat16 [768, 3072], P('fsdp')
- contract_grad: float32 [3072, 768], P('fsdp')
- contract_moment_new: float32 [3072, 768], P('fsdp')
- contract_weight_new: float32 [3072, 768], P('fsdp')
- contract_average_new: float32 [3072, 768], P('fsdp')
- contract_weight_low: bfloat16 [3072, 768], P('fsdp')
- vector_grad: float32 [10, 768], P(None, 'fsdp')
- vector_moment_new: float32 [10, 768], P(None, 'fsdp')
- vector_weight_new: float32 [10, 768], P(None, 'fsdp')
- vector_average_new: float32 [10, 768], P(None, 'fsdp')
- vector_weight_low: bfloat16 [10, 768], P(None, 'fsdp')
Inputs may be any that keep to these rules, and one draw needn't show every extreme that they name: `slot_clip`: slots of one device hold whole clips one after another, then its empty slots (-1); equal numbers stand only on one device; a clip has at most 8 frames, and some clip has exactly 8; each device has 12 or more live slots, and some device has no empty one. `vector_weight`: rows 0 and 3 lie within 0.4 to 1.6, the others within -1.2 to 1.2. `vector_average`: rows 0 and 3 lie within 0.4 to 1.6, the others within -1.2 to 1.2.
All inputs are finite; a program needn't handle non-finite values.
Results may differ from a plain program's by a relative error of at most 0.015.
Values may be sent and summed in bfloat16 or wider, within the bound.
A program may use at most 192 MiB of HBM per device.

v0:
```python
from functools import partial

import jax
import jax.numpy as jnp
from jax import lax
from jax.sharding import PartitionSpec as P

HEADS = 12
HEAD_DIM = 64


EPSILON = 1e-06
MOMENTUM = 0.5
AVERAGE = 0.5
RATES = (0.3, 0.3, 0.1, 0.03, 0.5)
NEGATIVE = -1e30


def norm_apply(values, gain, shift):
    row_mean = jnp.mean(values, axis=-1, keepdims=True)
    centred = values - row_mean
    spread = jnp.mean(centred * centred, axis=-1, keepdims=True)
    return centred * lax.rsqrt(spread + EPSILON) * gain + shift


def head_split(matrix):
    return jnp.swapaxes(matrix.reshape(matrix.shape[0], HEADS, HEAD_DIM), 0, 1)


def head_merge(stacked):
    return jnp.swapaxes(stacked, 0, 1).reshape(stacked.shape[1], HEADS * HEAD_DIM)


def masked_scores(query, keys, allowed):
    scores = jnp.einsum("qd,kd->qk", query, keys, preferred_element_type=jnp.float32)
    return jnp.where(allowed, scores, NEGATIVE)


def head_forward(allowed, pieces):
    query, keys, values = pieces
    scores = masked_scores(query, keys, allowed)
    row_top = jnp.max(scores, axis=-1, keepdims=True)
    total = jnp.sum(jnp.exp(scores - row_top), axis=-1, keepdims=True)
    log_total = row_top + jnp.log(total)
    probs_low = jnp.exp(scores - log_total).astype(jnp.bfloat16)
    mixed = jnp.dot(probs_low, values, preferred_element_type=jnp.float32)
    return (mixed, log_total)


def head_backward(allowed, pieces):
    query, keys, values, log_total, upstream = pieces
    scores = masked_scores(query, keys, allowed)
    probs = jnp.exp(scores - log_total)
    from_out = jnp.einsum("qd,kd->qk", upstream, values, preferred_element_type=jnp.float32)
    value_grad = jnp.einsum(
        "qk,qd->kd", probs.astype(jnp.bfloat16), upstream, preferred_element_type=jnp.float32
    )
    inner = jnp.sum(from_out * probs, axis=-1, keepdims=True)
    score_grad = (probs * (from_out - inner)).astype(jnp.bfloat16)
    query_grad = jnp.dot(score_grad, keys, preferred_element_type=jnp.float32)
    key_grad = jnp.einsum("qk,qd->kd", score_grad, query, preferred_element_type=jnp.float32)
    return (query_grad, key_grad, value_grad)


def on_device(
    patches,
    slot_clip,
    out_grad,
    project_in_weight,
    project_in_moment,
    project_in_average,
    project_out_weight,
    project_out_moment,
    project_out_average,
    expand_weight,
    expand_moment,
    expand_average,
    contract_weight,
    contract_moment,
    contract_average,
    vector_weight,
    vector_moment,
    vector_average,
):
    masters = (project_in_weight, project_out_weight, expand_weight, contract_weight, vector_weight)
    moments = (project_in_moment, project_out_moment, expand_moment, contract_moment, vector_moment)
    averages = (
        project_in_average,
        project_out_average,
        expand_average,
        contract_average,
        vector_average,
    )
    lowered = tuple((master.astype(jnp.bfloat16) for master in masters))
    inward_full, outward_full, expand_full, contract_full, vector_full = (
        lax.all_gather(lowered[0], "fsdp", axis=0, tiled=True),
        lax.all_gather(lowered[1], "fsdp", axis=0, tiled=True),
        lax.all_gather(lowered[2], "fsdp", axis=0, tiled=True),
        lax.all_gather(lowered[3], "fsdp", axis=0, tiled=True),
        lax.all_gather(lowered[4], "fsdp", axis=1, tiled=True),
    )
    model_width = patches.shape[1]
    residual_in = patches.astype(jnp.float32)
    row_count = residual_in.shape[0]
    token_clip = jnp.repeat(slot_clip, row_count // slot_clip.shape[0])
    live_rows = (token_clip >= 0).astype(jnp.float32)[:, None]
    positions = jnp.arange(row_count)
    allowed = (token_clip[:, None] == token_clip[None, :]) & (token_clip[None, :] >= 0) | (
        positions[:, None] == positions[None, :]
    )
    vector_wide = vector_full.astype(jnp.float32)
    bias_out = vector_wide[2]
    bias_last = vector_wide[5]
    bias_expand = vector_wide[6:].reshape(-1)
    normed_low = norm_apply(residual_in, vector_wide[0], vector_wide[1]).astype(jnp.bfloat16)
    triple = jnp.dot(normed_low, inward_full, preferred_element_type=jnp.float32)
    scale = HEAD_DIM ** (-0.5)
    query_heads = head_split((triple[:, :model_width] * scale).astype(jnp.bfloat16))
    key_heads = head_split(triple[:, model_width : 2 * model_width].astype(jnp.bfloat16))
    value_heads = head_split(triple[:, 2 * model_width :].astype(jnp.bfloat16))
    mixed_heads, log_totals = lax.map(
        partial(head_forward, allowed), (query_heads, key_heads, value_heads)
    )
    mixed_low = head_merge(mixed_heads).astype(jnp.bfloat16)
    middle = residual_in + (
        jnp.dot(mixed_low, outward_full, preferred_element_type=jnp.float32) + bias_out
    )
    normed_two_low = norm_apply(middle, vector_wide[3], vector_wide[4]).astype(jnp.bfloat16)
    before = jnp.dot(normed_two_low, expand_full, preferred_element_type=jnp.float32) + bias_expand
    hidden_low = jax.nn.gelu(before, approximate=False).astype(jnp.bfloat16)
    final = middle + (
        jnp.dot(hidden_low, contract_full, preferred_element_type=jnp.float32) + bias_last
    )
    block_out = final.astype(jnp.bfloat16)
    inward_back, outward_back, expand_back, contract_back, vector_back = (
        lax.all_gather(lowered[0], "fsdp", axis=0, tiled=True),
        lax.all_gather(lowered[1], "fsdp", axis=0, tiled=True),
        lax.all_gather(lowered[2], "fsdp", axis=0, tiled=True),
        lax.all_gather(lowered[3], "fsdp", axis=0, tiled=True),
        lax.all_gather(lowered[4], "fsdp", axis=1, tiled=True),
    )
    vector_again = vector_back.astype(jnp.float32)
    upstream = out_grad.astype(jnp.float32) * live_rows
    upstream_low = upstream.astype(jnp.bfloat16)
    last_bias_grad = jnp.sum(upstream, axis=0)
    contract_grad = jnp.einsum(
        "rf,rd->fd", hidden_low, upstream_low, preferred_element_type=jnp.float32
    )
    hidden_grad = jnp.einsum(
        "rd,fd->rf", upstream_low, contract_back, preferred_element_type=jnp.float32
    )
    gelu_value, gelu_back = jax.vjp(partial(jax.nn.gelu, approximate=False), before)
    before_low = gelu_back(hidden_grad)[0].astype(jnp.bfloat16)
    expand_bias_grad = jnp.sum(before_low.astype(jnp.float32), axis=0)
    expand_grad = jnp.einsum(
        "rd,rf->df", normed_two_low, before_low, preferred_element_type=jnp.float32
    )
    normed_two_grad = jnp.einsum(
        "rf,df->rd", before_low, expand_back, preferred_element_type=jnp.float32
    )
    norm_value, norm_two_back = jax.vjp(norm_apply, middle, vector_again[3], vector_again[4])
    middle_part, gain_two_grad, shift_two_grad = norm_two_back(normed_two_grad)
    middle_grad = upstream + middle_part
    branch_low = middle_grad.astype(jnp.bfloat16)
    out_bias_grad = jnp.sum(branch_low.astype(jnp.float32), axis=0)
    outward_grad = jnp.einsum(
        "re,rd->ed", mixed_low, branch_low, preferred_element_type=jnp.float32
    )
    mixed_grad = jnp.einsum(
        "rd,ed->re", branch_low, outward_back, preferred_element_type=jnp.float32
    ).astype(jnp.bfloat16)
    upstream_heads = head_split(mixed_grad)
    query_grad, key_grad, value_grad = lax.map(
        partial(head_backward, allowed),
        (query_heads, key_heads, value_heads, log_totals, upstream_heads),
    )
    triple_grad = jnp.concatenate(
        [
            head_merge(query_grad).astype(jnp.bfloat16) * scale,
            head_merge(key_grad).astype(jnp.bfloat16),
            head_merge(value_grad).astype(jnp.bfloat16),
        ],
        axis=1,
    )
    inward_grad = jnp.einsum(
        "rd,re->de", normed_low, triple_grad, preferred_element_type=jnp.float32
    )
    normed_one_grad = jnp.einsum(
        "re,de->rd", triple_grad, inward_back, preferred_element_type=jnp.float32
    )
    norm_first, norm_one_back = jax.vjp(norm_apply, residual_in, vector_again[0], vector_again[1])
    input_part, gain_one_grad, shift_one_grad = norm_one_back(normed_one_grad)
    patch_grad = middle_grad + input_part
    vector_grad = jnp.concatenate(
        [
            jnp.stack(
                [
                    gain_one_grad,
                    shift_one_grad,
                    out_bias_grad,
                    gain_two_grad,
                    shift_two_grad,
                    last_bias_grad,
                ]
            ),
            expand_bias_grad.reshape(4, -1),
        ],
        axis=0,
    )
    local_grads = (inward_grad, outward_grad, expand_grad, contract_grad, vector_grad)
    shard_grads = (
        lax.psum_scatter(local_grads[0], "fsdp", scatter_dimension=0, tiled=True),
        lax.psum_scatter(local_grads[1], "fsdp", scatter_dimension=0, tiled=True),
        lax.psum_scatter(local_grads[2], "fsdp", scatter_dimension=0, tiled=True),
        lax.psum_scatter(local_grads[3], "fsdp", scatter_dimension=0, tiled=True),
        lax.psum_scatter(local_grads[4], "fsdp", scatter_dimension=1, tiled=True),
    )
    total_grads = (
        lax.psum(shard_grads[0].astype(jnp.bfloat16), "rep").astype(jnp.float32),
        lax.psum(shard_grads[1].astype(jnp.bfloat16), "rep").astype(jnp.float32),
        lax.psum(shard_grads[2].astype(jnp.bfloat16), "rep").astype(jnp.float32),
        lax.psum(shard_grads[3].astype(jnp.bfloat16), "rep").astype(jnp.float32),
        lax.psum(shard_grads[4].astype(jnp.bfloat16), "rep").astype(jnp.float32),
    )
    tokens_all = row_count * lax.axis_size("fsdp") * lax.axis_size("rep")
    outputs = [block_out, patch_grad]
    for member in range(5):
        grad_sum = total_grads[member]
        rate = RATES[member] / tokens_all**0.5
        moment_new = MOMENTUM * moments[member] + grad_sum
        weight_new = masters[member] - rate * (grad_sum + MOMENTUM * moment_new)
        average_new = AVERAGE * averages[member] + (1.0 - AVERAGE) * weight_new
        outputs.extend(
            [grad_sum, moment_new, weight_new, average_new, weight_new.astype(jnp.bfloat16)]
        )
    return tuple(outputs)


def solution(mesh):
    in_specs = (
        P(("fsdp", "rep"), None),
        P(("fsdp", "rep")),
        P(("fsdp", "rep"), None),
        P("fsdp", None),
        P("fsdp", None),
        P("fsdp", None),
        P("fsdp", None),
        P("fsdp", None),
        P("fsdp", None),
        P("fsdp", None),
        P("fsdp", None),
        P("fsdp", None),
        P("fsdp", None),
        P("fsdp", None),
        P("fsdp", None),
        P(None, "fsdp"),
        P(None, "fsdp"),
        P(None, "fsdp"),
    )
    out_specs = (
        P(("fsdp", "rep"), None),
        P(("fsdp", "rep"), None),
        P("fsdp", None),
        P("fsdp", None),
        P("fsdp", None),
        P("fsdp", None),
        P("fsdp", None),
        P("fsdp", None),
        P("fsdp", None),
        P("fsdp", None),
        P("fsdp", None),
        P("fsdp", None),
        P("fsdp", None),
        P("fsdp", None),
        P("fsdp", None),
        P("fsdp", None),
        P("fsdp", None),
        P("fsdp", None),
        P("fsdp", None),
        P("fsdp", None),
        P("fsdp", None),
        P("fsdp", None),
        P(None, "fsdp"),
        P(None, "fsdp"),
        P(None, "fsdp"),
        P(None, "fsdp"),
        P(None, "fsdp"),
    )
    return jax.shard_map(
        on_device, mesh=mesh, in_specs=in_specs, out_specs=out_specs, check_vma=False
    )
```

profile of v0, /device:TPU:0, one launch (start us, length us, event | category | flops | bytes accessed | tf_op | source)
XLA Modules:
  0.0 1104.3 jit_solution(13820761838799056083)
XLA Ops:
  14.4 32.4 %all-gather = bf16[8,96,10]{1,2,0:T(8,128)(2,1)S(1)} all-gather(bf16[1,96,10]{1,2,0:T(8,128)(2,1)S(1)} %convert_bitcast_fusion), channel_id=1, replica_groups=mesh['fsdp'=8,'rep'=4] {'fsdp'}, dimensions={0}, use_global_device_ids=true | all-gather | bytes 17280 | tf_op jit(solution)/shard_map/all_gather | solution.py:100
  49.9 29.0 %all-gather.6.cloned.1.call-done = bf16[768,2304]{1,0:T(8,128)(2,1)} async-done(((bf16[96,2304]{1,0:T(8,128)(2,1)}), bf16[768,2304]{1,0:T(8,128)(2,1)}) %all-gather.6.cloned.1.call-update) | async-done | bytes 3538960 | tf_op jit(solution)/shard_map/all_gather | solution.py:96
  78.9 9.5 fusion.99
  94.5 4.7 copy.78
  103.1 4.6 copy.79
  115.2 4.6 copy.77
  121.2 97.4 %while.28 = (s32[]{:T(128)}, bf16[12,1176,64]{1,2,0:T(8,128)(2,1)}, f32[12,1176,1]{1,2,0:T(1,128)}, bf16[12,1176,64]{2,1,0:T(8,128)(2,1)}, bf16[12,1176,64]{2,1,...) while((s32[]{:T(128)}, bf16[12,1176,64]{1,2,0:T(8,128)(2,1)}, ...), condition=%wide.region_5.6_spmd.clone, body=%wide.region_2.5_spmd.clone.sunk | while | flops 367870432 | bytes 17890396 | solution.py:121
  225.4 40.8 %multiply_convert_fusion.1 = (bf16[1176,3072]{1,0:T(8,128)(2,1)}, f32[1176,3072]{1,0:T(8,128)}, f32[1176,3072]{1,0:T(8,128)}) fusion(f32[3072]{0:T(1024)S(1)} %add.190, bf16[768,3072]{1,0:T(8,128)(2,1)} %all-gather.10.cloned.1.call-done, f32[1176,768]{1,0:T(8,128)} %copy-done.4, f32[768]{0:T(1024)S(1)} %get-tuple-element.235, ...), kind=kOutput, calls=%fused_computation.61 | convolution fusion | flops 5792016384 | bytes 44485824 | tf_op jit(solution)/shard_map/dot_general | solution.py:129
  266.2 17.2 %all-gather.12.cloned.1.call-done = bf16[3072,768]{1,0:T(8,128)(2,1)} async-done(((bf16[384,768]{1,0:T(8,128)(2,1)}), bf16[3072,768]{1,0:T(8,128)(2,1)}) %all-gather.12.cloned.1.call-update) | async-done | bytes 4718608 | tf_op jit(solution)/shard_map/all_gather | solution.py:99
  283.4 19.6 %convert_reduce_fusion = (f32[3072]{0:T(1024)}, bf16[1176,3072]{1,0:T(8,128)(2,1)}) fusion(f32[1176,3072]{1,0:T(8,128)} %get-tuple-element.309, f32[1176,3072]{1,0:T(8,128)} %get-tuple-element.322, bf16[3072,768]{1,0:T(8,128)(2,1)} %all-gather.12.cloned.1.call-done, bf16[1176,768]{1,0:T(8,128)(2,1)S(1)} %copy-done.6, f32[1176]{0:T(1024)S(1)} %copy-done.36), kind=kOutput, calls=%fused_computation.59 | convolution fusion | flops 5609573376 | bytes 42668640 | tf_op jit(solution)/shard_map/rd,fd->rf/dot_general | solution.py:149
  303.0 13.0 %multiply_reduce_fusion.1 = (f32[768]{0:T(1024)}, f32[1176]{0:T(1024)S(1)}, f32[768]{0:T(1024)}, f32[1176,768]{1,0:T(8,128)S(1)}) fusion(f32[1176,768]{1,0:T(8,128)} %copy-done.4, f32[1176]{0:T(1024)S(1)} %fusion.79, f32[1176]{0:T(1024)S(1)} %broadcast_multiply_fusion, f32[768]{0:T(1024)S(1)} %get-tuple-element.236, ...), kind=kOutput, calls=%fused_computation.98 | convolution fusion | flops 5556286464 | bytes 19192608 | tf_op jit(solution)/shard_map/rf,df->rd/dot_general | solution.py:158
  323.6 4.3 convolution_convert_fusion
  335.1 161.5 %while.29 = (s32[]{:T(128)}, bf16[12,1176,64]{1,2,0:T(8,128)(2,1)}, bf16[12,1176,64]{1,2,0:T(8,128)(2,1)}, bf16[12,1176,64]{1,2,0:T(8,128)(2,1)}, bf16[12,1176,6...) while((s32[]{:T(128)}, bf16[12,1176,64]{1,2,0:T(8,128)(2,1)}, ...), condition=%wide.region_12.13_spmd.clone, body=%wide.region_10.12_spmd.clone.sunk | while | flops 901699136 | bytes 45334392 | solution.py:173
  499.8 10.0 fusion.72
  510.5 12.9 %fusion.86 = f32[768,3072]{1,0:T(8,128)} fusion(bf16[1176,3072]{1,0:T(8,128)(2,1)} %get-tuple-element.326, f32[1176,768]{1,0:T(8,128)} %copy-done.4, f32[768]{0:T(1024)S(1)} %copy-done.56, f32[768]{0:T(1024)S(1)} %get-tuple-element.236, f32[1176]{0:T(1024)S(1)} %fusion.79, f32[1176]{0:T(1024)S(1)} %broadcast_multiply_fusion), kind=kOutput, calls=%fused_computation.153 | convolution fusion | flops 5553580032 | bytes 20290752 | tf_op jit(solution)/shard_map/rd,rf->df/dot_general | solution.py:155
  523.5 11.8 %fusion.75 = f32[3072,768]{1,0:T(8,128)} fusion(bf16[1176,3072]{1,0:T(8,128)(2,1)} %get-tuple-element.308, bf16[1176,768]{1,0:T(8,128)(2,1)} %param.24, f32[1176]{0:T(1024)S(1)} %copy-done.36), kind=kOutput, calls=%fused_computation.123 | convolution fusion | flops 5551773696 | bytes 18473568 | tf_op jit(solution)/shard_map/rf,rd->fd/dot_general | solution.py:146
  535.3 9.2 fusion.87
  554.0 83.2 %reduce-scatter.8.cloned.1.call-done = f32[96,2304]{1,0:T(8,128)} async-done(((f32[768,2304]{1,0:T(8,128)}), f32[96,2304]{1,0:T(8,128)}) %reduce-scatter.8.cloned.1.call-update) | async-done | bytes 884752 | tf_op jit(solution)/shard_map/reduce_scatter | solution.py:212
  639.1 164.6 %reduce-scatter.12.cloned.1.call-done = f32[96,3072]{1,0:T(8,128)} async-done(((f32[768,3072]{1,0:T(8,128)}), f32[96,3072]{1,0:T(8,128)}) %reduce-scatter.12.cloned.1.call-update) | async-done | bytes 1179664 | tf_op jit(solution)/shard_map/reduce_scatter | solution.py:214
  805.9 164.4 %reduce-scatter.14.cloned.1.call-done = f32[384,768]{1,0:T(8,128)} async-done(((f32[3072,768]{1,0:T(8,128)}), f32[384,768]{1,0:T(8,128)}) %reduce-scatter.14.cloned.1.call-update) | async-done | bytes 1179664 | tf_op jit(solution)/shard_map/reduce_scatter | solution.py:215
  972.5 11.0 fusion.71
  983.6 51.4 %reduce-scatter.16.cloned.1.call-done = f32[96,10]{1,0:T(8,128)} async-done(((f32[768,10]{1,0:T(8,128)}), f32[96,10]{1,0:T(8,128)}) %reduce-scatter.16.cloned.1.call-update) | async-done | bytes 3856
  1035.9 6.3 psum.39
  1044.7 40.3 %all-reduce.3.cloned.1.call-done = (bf16[96,2304]{1,0:T(8,128)(2,1)}, bf16[96,768]{1,0:T(8,128)(2,1)}, bf16[96,3072]{1,0:T(8,128)(2,1)}, bf16[384,768]{1,0:T(8,128)(2,1)}) async-done(((bf16[96,2304]{1,0:T(8,128)(2,1)}, bf16[96,768]{1,0:T(8,128)(2,1)}, bf16[96,3072]{1,0:T(8,128)(2,1)}, bf16[384,768]{1,0:T(8,128)(2,1)}), (bf16[96,2304]{1,0:T(8,128)(2,1)}, bf16[96,768]{1,0:T(8,128)(2,1)}, ...) | async-done | bytes 1769488 | tf_op jit(solution)/shard_map/psum | solution.py:219
  (359 shorter events, 343.8 us)
Async XLA Ops:
  7.2 40.3 %copy-start.2 = (bf16[1176,768]{1,0:T(8,128)(2,1)S(1)}, bf16[1176,768]{1,0:T(8,128)(2,1)}, u32[]{:S(2)}) copy-start(bf16[1176,768]{1,0:T(8,128)(2,1)} %param.22) | copy-start | bytes 5419012
  7.2 71.7 %all-gather.6.cloned.1.call-start = ((), (), s32[]{:S(2)}) async-start(), calls=%async_computation.5 | async-start | bytes 3981312 | tf_op jit(solution)/shard_map/all_gather | solution.py:96
  9.4 209.2 %all-gather.8.cloned.1.call-start = ((), (), s32[]{:S(2)}) async-start(), calls=%async_computation.6 | async-start | bytes 1327104 | tf_op jit(solution)/shard_map/all_gather | solution.py:97
  11.2 214.2 %all-gather.10.cloned.1.call-start = ((), (), s32[]{:S(2)}) async-start(), calls=%async_computation.7 | async-start | bytes 5308416 | tf_op jit(solution)/shard_map/all_gather | solution.py:98
  13.4 270.0 %all-gather.12.cloned.1.call-start = ((), (), s32[]{:S(2)}) async-start(), calls=%async_computation.8 | async-start | bytes 5308416 | tf_op jit(solution)/shard_map/all_gather | solution.py:99
  14.3 538.0 %reduce-scatter.10.cloned.1.call-start = ((), (), s32[]{:S(2)}) async-start(), calls=%async_computation.10 | async-start | bytes 2654208 | tf_op jit(solution)/shard_map/reduce_scatter | solution.py:213
  47.5 41.0 %copy-start.43 = (f32[768]{0:T(1024)}, f32[768]{0:T(1024)S(1)}, u32[]{:S(2)}) copy-start(f32[768]{0:T(1024)S(1)} %get-tuple-element.239) | copy-start | bytes 9220
  47.5 41.0 %copy-start.57 = (f32[768]{0:T(1024)}, f32[768]{0:T(1024)S(1)}, u32[]{:S(2)}) copy-start(f32[768]{0:T(1024)S(1)} %get-tuple-element.238) | copy-start | bytes 9220
  47.5 177.9 %copy-start.55 = (f32[768]{0:T(1024)}, f32[768]{0:T(1024)S(1)}, u32[]{:S(2)}) copy-start(f32[768]{0:T(1024)S(1)} %get-tuple-element.235) | copy-start | bytes 9220
  47.9 40.6 %copy-start.32 = (f32[1176]{0:T(1024)}, f32[1176]{0:T(1024)S(1)}, u32[]{:S(2)}) copy-start(f32[1176]{0:T(1024)S(1)} %broadcast_multiply_fusion.1) | copy-start | bytes 14116
  49.1 39.3 %copy-start.34 = (f32[1176]{0:T(1024)}, f32[1176]{0:T(1024)S(1)}, u32[]{:S(2)}) copy-start(f32[1176]{0:T(1024)S(1)} %fusion.78) | copy-start | bytes 14116
  225.4 58.0 %copy-start.6 = (bf16[1176,768]{1,0:T(8,128)(2,1)S(1)}, bf16[1176,768]{1,0:T(8,128)(2,1)}, u32[]{:S(2)}) copy-start(bf16[1176,768]{1,0:T(8,128)(2,1)} %param.24) | copy-start | bytes 5419012
  225.4 58.0 %copy-start.36 = (f32[1176]{0:T(1024)S(1)}, f32[1176]{0:T(1024)}, u32[]{:S(2)}) copy-start(f32[1176]{0:T(1024)} %get-tuple-element.306) | copy-start | bytes 14116
  330.6 306.5 %reduce-scatter.8.cloned.1.call-start = ((), (), s32[]{:S(2)}) async-start(), calls=%async_computation.9 | async-start | bytes 7962624 | tf_op jit(solution)/shard_map/reduce_scatter | solution.py:212
  509.9 293.9 %reduce-scatter.12.cloned.1.call-start = ((), (), s32[]{:S(2)}) async-start(), calls=%async_computation.11 | async-start | bytes 10616832 | tf_op jit(solution)/shard_map/reduce_scatter | solution.py:214
  523.4 446.9 %reduce-scatter.14.cloned.1.call-start = ((), (), s32[]{:S(2)}) async-start(), calls=%async_computation.12 | async-start | bytes 10616832 | tf_op jit(solution)/shard_map/reduce_scatter | solution.py:215
  535.3 499.7 %reduce-scatter.16.cloned.1.call-start = ((), (), s32[]{:S(2)}) async-start(), calls=%async_computation.13 | async-start | bytes 442368
  552.0 420.5 %copy-start.54 = (f32[768]{0:T(1024)S(1)}, f32[768]{0:T(1024)}, u32[]{:S(2)}) copy-start(f32[768]{0:T(1024)} %get-tuple-element.234) | copy-start | bytes 9220
  552.0 533.1 %all-reduce.3.cloned.1.call-start = ((), (), s32[]{:S(2)}) async-start(), calls=%async_computation.14 | async-start | bytes 3538944 | tf_op jit(solution)/shard_map/psum | solution.py:219
  972.5 69.6 %copy-start.49 = (f32[10,96]{1,0:T(8,128)S(1)}, f32[10,96]{1,0:T(8,128)}, u32[]{:S(2)}) copy-start(f32[10,96]{1,0:T(8,128)} %param.37) | copy-start | bytes 11524
  972.5 112.6 %copy-start.11 = (f32[384,768]{1,0:T(8,128)S(1)}, f32[384,768]{1,0:T(8,128)}, u32[]{:S(2)}) copy-start(f32[384,768]{1,0:T(8,128)} %param.34) | copy-start | bytes 3538948
  972.5 112.5 %copy-start.19 = (f32[384,768]{1,0:T(8,128)S(1)}, f32[384,768]{1,0:T(8,128)}, u32[]{:S(2)}) copy-start(f32[384,768]{1,0:T(8,128)} %param.35) | copy-start | bytes 3538948
  983.6 104.6 %copy-start.20 = (f32[384,768]{1,0:T(8,128)S(1)}, f32[384,768]{1,0:T(8,128)}, u32[]{:S(2)}) copy-start(f32[384,768]{1,0:T(8,128)} %param.36) | copy-start | bytes 3538948
  1043.4 46.0 %copy-start.47 = (f32[10,96]{1,0:T(8,128)}, f32[10,96]{1,0:T(8,128)S(1)}, u32[]{:S(2)}) copy-start(f32[10,96]{1,0:T(8,128)S(1)} %get-tuple-element.283) | copy-start | bytes 11524
  (49 other events, 206.7 us)
Sparse Core Ops, SparseCore 0:
  10.8 68.0 all-gather.5
  81.7 39.5 all-gather.7
  124.0 78.6 all-gather.9
  205.4 77.9 all-gather.11
  330.8 67.0 reduce-scatter.9
  510.0 127.1 reduce-scatter.7
  641.2 162.5 reduce-scatter.11
  807.8 162.5 reduce-scatter.13
  974.5 60.4 reduce-scatter.15
  1039.4 45.6 all-reduce.2
where the time goes:
time: 1120 us; the launch traced here: 1100 us
  waiting for transfers between devices  550 us (49%)
  matrix products  370 us (33%)
  other arithmetic  67 us (6%)
  local copies, waits for them, and re-layouts  62.2 us (6%)
  blocking collectives  38.6 us (3%)
  between operations  15.3 us (1%)
    reduce_scatter x1, waiting for transfers between devices, on_device(): lax.psum_scatter(local_grads[2], 'fsdp', scatter_dimension=0, tiled=True)  165 us
    reduce_scatter x1, waiting for transfers between devices, on_device(): lax.psum_scatter(local_grads[3], 'fsdp', scatter_dimension=0, tiled=True)  164 us
    reduce_scatter x1, waiting for transfers between devices, on_device(): lax.psum_scatter(local_grads[0], 'fsdp', scatter_dimension=0, tiled=True)  83.2 us
    dot_general x24, matrix products, masked_scores(): jnp.einsum('qd,kd->qk', query, keys, preferred_element_type=jnp.float32)  83 us
    unnamed x11, waiting for transfers between devices  51.6 us
    dot_general x1, matrix products, on_device(): jnp.dot(normed_two_low, expand_full, preferred_element_type=jnp.float32)  40.8 us
    psum x1, waiting for transfers between devices, on_device(): lax.psum(shard_grads[0].astype(jnp.bfloat16), 'rep').astype(jnp.float32)  40.3 us
    dot_general x12, matrix products, head_forward(): mixed = jnp.dot(probs_low, values, preferred_element_type=jnp.float32)  32.5 us
  transfers between devices with their start and end apart: 10, of which 7 were waited for; matrix products, arithmetic and copies ran while one was open for 39% of the time, Pallas kernels for 0%

commit v1 on v0

v1 whole, which is shorter than its diff:
```python
import functools
import math

import jax
import jax.numpy as jnp
from jax import lax
from jax.sharding import PartitionSpec as P
import jax.experimental.pallas as pl
import jax.experimental.pallas.tpu as pltpu

BF, F32 = jnp.bfloat16, jnp.float32
HEAD_DIM = 64
SLOT = 49
LIVE_MAX = 8
WIN = 416
EPSILON = 1e-06
MOMENTUM = 0.5
AVERAGE = 0.5
RATES = (0.3, 0.3, 0.1, 0.03, 0.5)
NEG = -1e30

def dg(a,b,ca,cb):
    return lax.dot_general(a,b,(((ca,),(cb,)),((),())),preferred_element_type=F32)

def group_end(clips, start, slots):
    end = start+1
    for e in range(2, LIVE_MAX+1):
        cand = start+e
        safe = jnp.minimum(cand, slots-1)
        edge = (cand == slots) | ((cand < slots) & ((clips[safe] != clips[jnp.maximum(safe-1,0)]) | (clips[safe] < 0)))
        end = jnp.where(edge, cand, end)
    return end

def fill_bias(clips, w0, slots, bias):
    def keys(shape, dim):
        row = lax.broadcasted_iota(jnp.int32, shape, dim) + w0
        slot = (row*1338) >> 16
        def one(s, key):
            return jnp.where((slot == s) & (clips[s] >= 0), clips[s], key)
        return lax.fori_loop(0, slots, one, -1-row, unroll=True)
    bias[...] = jnp.where(keys((WIN,1),0) == keys((1,WIN),1), 0.0, NEG)

def clear_tail(ref, slots):
    tail = slots*SLOT//16*16
    ref[pl.ds(tail, ref.shape[0]-tail), :] = jnp.zeros((ref.shape[0]-tail, ref.shape[1]), BF)

def fwd_kernel(clips, t_ref, o_ref, bias):
    slots = clips.shape[0]
    rows = t_ref.shape[0]; D = o_ref.shape[1]
    clear_tail(o_ref, slots)
    def group(g, start):
        @pl.when(start < slots)
        def _():
            end = group_end(clips, start, slots)
            r0 = start*SLOT; r1 = end*SLOT
            w0 = pl.multiple_of(jnp.minimum((r0>>4)<<4, rows-WIN), 16)
            fill_bias(clips, w0, slots, bias)
            rowi = lax.broadcasted_iota(jnp.int32,(WIN,128),0)+w0
            mine = (rowi >= r0) & (rowi < r1)
            lane = lax.broadcasted_iota(jnp.int32,(1,128),1)
            win = pl.ds(w0, WIN)
            for p in range(D//128):
                q = t_ref[win, pl.ds(p*128,128)]
                k = t_ref[win, pl.ds(D+p*128,128)]
                v = t_ref[win, pl.ds(2*D+p*128,128)]
                outs=[]
                for h in range(2):
                    keep = (lane//64 == h).astype(BF)
                    s = dg(q*keep, k, 1, 1) + bias[...]
                    top = jnp.max(s, axis=1, keepdims=True)
                    e = jnp.exp(s-top)
                    inv = 1.0/jnp.sum(e, axis=1, keepdims=True)
                    pl_ = (e*inv).astype(BF)
                    outs.append(jnp.dot(pl_, v, preferred_element_type=F32))
                o = jnp.where(lane < 64, outs[0], outs[1])
                old = o_ref[win, pl.ds(p*128,128)]
                o_ref[win, pl.ds(p*128,128)] = jnp.where(mine, o, old.astype(F32)).astype(BF)
        return jnp.where(start < slots, group_end(clips, start, slots), start)
    lax.fori_loop(0, (2*slots)//(LIVE_MAX+1)+1, group, 0)

def bwd_kernel(clips, t_ref, do_ref, dt_ref, bias):
    slots = clips.shape[0]
    rows = t_ref.shape[0]; D = do_ref.shape[1]
    clear_tail(dt_ref, slots)
    def group(g, start):
        @pl.when(start < slots)
        def _():
            end = group_end(clips, start, slots)
            r0 = start*SLOT; r1 = end*SLOT
            w0 = pl.multiple_of(jnp.minimum((r0>>4)<<4, rows-WIN), 16)
            fill_bias(clips, w0, slots, bias)
            rowi = lax.broadcasted_iota(jnp.int32,(WIN,128),0)+w0
            mine = (rowi >= r0) & (rowi < r1)
            lane = lax.broadcasted_iota(jnp.int32,(1,128),1)
            win = pl.ds(w0, WIN)
            for p in range(D//128):
                q = t_ref[win, pl.ds(p*128,128)]
                k = t_ref[win, pl.ds(D+p*128,128)]
                v = t_ref[win, pl.ds(2*D+p*128,128)]
                do = do_ref[win, pl.ds(p*128,128)]
                dqs=[];dks=[];dvs=[]
                for h in range(2):
                    keep = (lane//64 == h).astype(BF)
                    s = dg(k, q*keep, 1, 1) + bias[...]
                    top = jnp.max(s, axis=0, keepdims=True)
                    e = jnp.exp(s-top)
                    inv = 1.0/jnp.sum(e, axis=0, keepdims=True)
                    pt = e*inv
                    dp = dg(v, do*keep, 1, 1)
                    dvs.append(jnp.dot(pt.astype(BF), do, preferred_element_type=F32))
                    inner = jnp.sum(dp*pt, axis=0, keepdims=True)
                    ds = (pt*(dp-inner)).astype(BF)
                    dks.append(jnp.dot(ds, q, preferred_element_type=F32))
                    dqs.append(dg(ds, k, 0, 0))
                for i,x in enumerate((dqs,dks,dvs)):
                    new = jnp.where(lane < 64, x[0], x[1]).astype(BF).astype(F32)
                    if i==0: new = new*(64**-0.5)
                    c = pl.ds(i*D+p*128,128)
                    old = dt_ref[win, c].astype(F32)
                    dt_ref[win, c] = jnp.where(mine, new, old).astype(BF)
        return jnp.where(start < slots, group_end(clips, start, slots), start)
    lax.fori_loop(0, (2*slots)//(LIVE_MAX+1)+1, group, 0)

def attend(clips, t):
    D=t.shape[1]//3
    return pl.pallas_call(fwd_kernel, out_shape=jax.ShapeDtypeStruct((t.shape[0],D),BF),
      in_specs=[pl.BlockSpec(memory_space=pltpu.SMEM), pl.BlockSpec(memory_space=pltpu.VMEM)],
      out_specs=pl.BlockSpec(memory_space=pltpu.VMEM),
      scratch_shapes=[pltpu.VMEM((WIN,WIN),F32)],
      compiler_params=pltpu.CompilerParams(vmem_limit_bytes=48*2**20),name="attention_forward")(clips,t)
def attend_back(clips, t, do):
    return pl.pallas_call(bwd_kernel, out_shape=jax.ShapeDtypeStruct(t.shape,BF),
      in_specs=[pl.BlockSpec(memory_space=pltpu.SMEM)]+[pl.BlockSpec(memory_space=pltpu.VMEM)]*2,
      out_specs=pl.BlockSpec(memory_space=pltpu.VMEM),
      scratch_shapes=[pltpu.VMEM((WIN,WIN),F32)],
      compiler_params=pltpu.CompilerParams(vmem_limit_bytes=48*2**20),name="attention_backward")(clips,t,do)


RT = 400


def dot_nt(left, right):
    return lax.dot_general(left, right, (((1,), (1,)), ((), ())), preferred_element_type=F32)


def dot_tn(left, right):
    return lax.dot_general(left, right, (((0,), (0,)), ((), ())), preferred_element_type=F32)


def dot_nn(left, right):
    return jnp.dot(left, right, preferred_element_type=F32)


def norm_parts(values):
    centred = values - jnp.mean(values, axis=-1, keepdims=True)
    scale = lax.rsqrt(jnp.mean(centred * centred, axis=-1, keepdims=True) + EPSILON)
    return centred * scale, scale


def norm_back(grad, gain, unit, scale):
    inner = grad * gain
    return scale * (
        inner
        - jnp.mean(inner, axis=-1, keepdims=True)
        - unit * jnp.mean(inner * unit, axis=-1, keepdims=True)
    )


def gelu_pair(u):
    bell = jnp.exp(-0.5 * u * u)
    t = 1.0 / (1.0 + (0.3275911 * 0.5**0.5) * jnp.abs(u))
    poly = t * (
        0.5 * 0.254829592
        + t * (-0.5 * 0.284496736 + t * (0.5 * 1.421413741 + t * (-0.5 * 1.453152027 + t * (0.5 * 1.061405429))))
    )
    tail = poly * bell
    phi = jnp.where(u < 0, tail, 1.0 - tail)
    return u * phi, phi + u * (bell * (2.0 * math.pi) ** -0.5)


def column_sum(values):
    return jnp.sum(values, axis=0, keepdims=True)


def tiles(rows, body):
    @pl.loop(0, rows // RT)
    def _(i):
        body(pl.ds(pl.multiple_of(i * RT, 16), RT))


def qkv_norm(x_ref, vec, a1_ref):
    def one(win):
        unit, _ = norm_parts(x_ref[win, :].astype(F32))
        a1_ref[win, :] = (unit * vec[0:1, :] + vec[1:2, :]).astype(BF)

    tiles(x_ref.shape[0], one)


def qkv_block(a1_ref, w_ref, t_ref, part):
    width = a1_ref.shape[1]

    def one(win):
        out = dot_nn(a1_ref[win, :], w_ref[...])
        if part == 0:
            out = out * HEAD_DIM**-0.5
        t_ref[win, pl.ds(part * width, width)] = out.astype(BF)

    tiles(a1_ref.shape[0], one)


def qkv_kernel(x_ref, vec, w_ref, t_ref, a1_ref):
    qkv_norm(x_ref, vec, a1_ref)
    for part in range(3):
        qkv_block(a1_ref, w_ref.at[part], t_ref, part)


def middle_step(x_ref, o_ref, vec, wo_ref, m_ref, a2_ref):
    def one(win):
        middle = x_ref[win, :].astype(F32) + (dot_nn(o_ref[win, :], wo_ref[...]) + vec[2:3, :])
        m_ref[win, :] = middle
        unit, _ = norm_parts(middle)
        a2_ref[win, :] = (unit * vec[3:4, :] + vec[4:5, :]).astype(BF)

    tiles(x_ref.shape[0], one)


def chunk_step(first, bias, a2_ref, dy_ref, we_ref, wc_ref, h_ref, du_ref, y_ref, da2_ref, be_ref):
    be_ref[...] = jnp.zeros_like(be_ref)

    def one(win):
        hidden, slope = gelu_pair(dot_nn(a2_ref[win, :], we_ref[...]) + bias)
        hidden = hidden.astype(BF)
        h_ref[win, :] = hidden
        du = (dot_nt(dy_ref[win, :], wc_ref[...]) * slope).astype(BF)
        du_ref[win, :] = du
        be_ref[...] += column_sum(du.astype(F32))
        y = dot_nn(hidden, wc_ref[...])
        da2 = dot_nt(du, we_ref[...])
        if first is True:
            y_ref[win, :] = y
            da2_ref[win, :] = da2
        else:
            y_ref[win, :] += y
            da2_ref[win, :] += da2

    tiles(a2_ref.shape[0], one)


def middle_back(live_rows, m_ref, y_ref, dy_ref, da2_ref, vec, wo_ref, out_ref, dm_ref, dz_ref, do_ref, sums):
    sums[...] = jnp.zeros_like(sums)

    def one(win):
        middle = m_ref[win, :]
        out_ref[win, :] = (middle + (y_ref[win, :] + vec[5:6, :])).astype(BF)
        unit, scale = norm_parts(middle)
        da2 = da2_ref[win, :]
        dy = dy_ref[win, :].astype(F32)
        dm = dy + norm_back(da2, vec[3:4, :], unit, scale)
        dm_ref[win, :] = dm
        dz = dm.astype(BF)
        dz_ref[win, :] = dz
        do_ref[win, :] = dot_nt(dz, wo_ref[...]).astype(BF)
        sums[0:1, :] += column_sum(da2 * unit)
        sums[1:2, :] += column_sum(da2)
        sums[2:3, :] += column_sum(dz.astype(F32))
        sums[3:4, :] += column_sum(dy)

    tiles(m_ref.shape[0], one)


def feed_kernel(
    x_ref, o_ref, dy_ref, vec, wo_ref, we_ref, wc_ref,
    out_ref, dm_ref, do_ref, gwo_ref, gwe_ref, gwc_ref, sums, be_ref,
    m_ref, a2_ref, h_ref, du_ref, y_ref, da2_ref, dz_ref,
):
    middle_step(x_ref, o_ref, vec, wo_ref, m_ref, a2_ref)
    for j in range(4):
        chunk_step(
            j == 0, vec[6 + j : 7 + j, :], a2_ref, dy_ref, we_ref.at[j], wc_ref.at[j],
            h_ref, du_ref, y_ref, da2_ref, be_ref.at[pl.ds(8 * j, 1)],
        )
        gwc_ref[j] = dot_tn(h_ref[...], dy_ref[...]).astype(BF)
        gwe_ref[j] = dot_tn(a2_ref[...], du_ref[...]).astype(BF)
    middle_back(None, m_ref, y_ref, dy_ref, da2_ref, vec, wo_ref, out_ref, dm_ref, dz_ref, do_ref, sums)
    gwo_ref[...] = dot_tn(o_ref[...], dz_ref[...]).astype(BF)


def first_back(x_ref, dt_ref, dm_ref, vec, w_refs, pg_ref, sums):
    sums[...] = jnp.zeros_like(sums)
    width = x_ref.shape[1]

    def one(win):
        da1 = dot_nt(dt_ref[win, pl.ds(0, width)], w_refs[0][...])
        da1 += dot_nt(dt_ref[win, pl.ds(width, width)], w_refs[1][...])
        da1 += dot_nt(dt_ref[win, pl.ds(2 * width, width)], w_refs[2][...])
        unit, scale = norm_parts(x_ref[win, :].astype(F32))
        pg_ref[win, :] = dm_ref[win, :] + norm_back(da1, vec[0:1, :], unit, scale)
        sums[0:1, :] += column_sum(da1 * unit)
        sums[1:2, :] += column_sum(da1)

    tiles(x_ref.shape[0], one)


def first_kernel(x_ref, a1_ref, dt_ref, dm_ref, vec, w_ref, pg_ref, gwi_ref, sums):
    width = x_ref.shape[1]
    for part in range(3):
        gwi_ref[part] = dot_tn(a1_ref[...], dt_ref[:, pl.ds(part * width, width)]).astype(BF)
    first_back(x_ref, dt_ref, dm_ref, vec, [w_ref.at[p] for p in range(3)], pg_ref, sums)


VM = pl.BlockSpec(memory_space=pltpu.VMEM)
SM = pl.BlockSpec(memory_space=pltpu.SMEM)


def vmem_call(kernel, name, ins, outs, scratch=(), smem=0):
    return pl.pallas_call(
        kernel,
        out_shape=[jax.ShapeDtypeStruct(s, d) for s, d in outs],
        in_specs=[SM] * smem + [VM] * (len(ins) - smem),
        out_specs=[VM] * len(outs),
        scratch_shapes=[pltpu.VMEM(s, d) for s, d in scratch],
        compiler_params=pltpu.CompilerParams(vmem_limit_bytes=60 * 2**20),
        name=name,
    )(*ins)


def run_qkv(x, vec, wi):
    rows, width = x.shape
    return vmem_call(
        qkv_kernel, "project_in", (x, vec, wi), [((rows, 3 * width), BF), ((rows, width), BF)]
    )


def run_feed(x, o, dy, vec, wo, we, wc):
    rows, width = x.shape
    wide, low = ((rows, width), F32), ((rows, width), BF)
    return vmem_call(
        feed_kernel, "feed_forward", (x, o, dy, vec, wo, we, wc),
        [low, wide, low, ((width, width), BF), ((4, width, width), BF), ((4, width, width), BF),
         ((8, width), F32), ((32, width), F32)],
        [wide, low, low, low, wide, wide, low],
    )


def run_first(x, a1, dt, dm, vec, wi):
    rows, width = x.shape
    return vmem_call(
        first_kernel, "project_in_back", (x, a1, dt, dm, vec, wi),
        [((rows, width), F32), ((3, width, width), BF), ((8, width), F32)],
    )


def pack_shards(wi, wo, we, wc, parts):
    rows, width = wo.shape
    wi = wi.reshape(rows, 3, width).swapaxes(0, 1)
    we = we.reshape(rows, parts, 4, rows).transpose(2, 0, 1, 3).reshape(4, rows, width)
    wc = wc.reshape(4, rows, width)
    return jnp.concatenate([wi, wo[None], we, wc], axis=0)


def unpack_shards(blocks, parts):
    rows, width = blocks.shape[1:]
    wi = blocks[0:3].swapaxes(0, 1).reshape(rows, 3 * width)
    we = blocks[4:8].reshape(4, rows, parts, rows).transpose(1, 2, 0, 3).reshape(rows, 4 * width)
    return wi, blocks[3], we, blocks[8:12].reshape(4 * rows, width)


def on_device(
    patches, slot_clip, out_grad,
    project_in_weight, project_in_moment, project_in_average,
    project_out_weight, project_out_moment, project_out_average,
    expand_weight, expand_moment, expand_average,
    contract_weight, contract_moment, contract_average,
    vector_weight, vector_moment, vector_average,
):
    masters = (project_in_weight, project_out_weight, expand_weight, contract_weight, vector_weight)
    moments = (project_in_moment, project_out_moment, expand_moment, contract_moment, vector_moment)
    averages = (project_in_average, project_out_average, expand_average, contract_average, vector_average)
    parts, copies = lax.axis_size("fsdp"), lax.axis_size("rep")
    mine, copy = lax.axis_index("fsdp"), lax.axis_index("rep")
    count, width = patches.shape
    rows = (count + RT - 1) // RT * RT
    sh = width // parts

    packed = pack_shards(*(m.astype(BF) for m in masters[:4]), parts).reshape(12 * sh, width)
    piece = 12 * sh // copies
    quarter = lax.dynamic_slice_in_dim(packed, copy * piece, piece, 0)
    full = lax.all_gather(quarter, ("fsdp", "rep"), axis=0, tiled=True)
    full = full.reshape(parts, 12, sh, width).swapaxes(0, 1).reshape(12, width, width)
    vec = lax.all_gather(vector_weight.astype(BF), "fsdp", axis=1, tiled=True).astype(F32)
    be = vec[6:].reshape(parts, 4, sh).swapaxes(0, 1).reshape(4, width)
    vec = jnp.concatenate([vec[:6], be, jnp.zeros((6, width), F32)], axis=0)

    pad = ((0, rows - count), (0, 0))
    live = jnp.repeat(slot_clip >= 0, SLOT)[:, None]
    x = jnp.pad(patches, pad)
    dy = jnp.pad(jnp.where(live, out_grad, 0), pad)
    t, a1 = run_qkv(x, vec, full[0:3])
    o = attend(slot_clip, t)
    out, dm, do, gwo, gwe, gwc, sums_two, sums_be = run_feed(x, o, dy, vec, full[3], full[4:8], full[8:12])
    dt = attend_back(slot_clip, t, do)
    pg, gwi, sums_one = run_first(x, a1, dt, dm, vec, full[0:3])

    grads = jnp.concatenate([gwi, gwo[None], gwe, gwc], axis=0)
    grads = grads.reshape(12, parts, sh, width).swapaxes(0, 1).reshape(parts * 12 * sh, width)
    grads = lax.psum_scatter(grads, ("fsdp", "rep"), scatter_dimension=0, tiled=True)
    grads = lax.all_gather(grads, "rep", axis=0, tiled=True).reshape(12, sh, width)
    be_grad = sums_be[::8].reshape(4, parts, sh).swapaxes(0, 1).reshape(4, width)
    vector = jnp.concatenate(
        [sums_one[0:2], sums_two[2:3], sums_two[0:2], sums_two[3:4], be_grad], axis=0
    )
    vector = lax.dynamic_slice_in_dim(lax.psum(vector, ("fsdp", "rep")), mine * sh, sh, 1)
    total_grads = tuple(g.astype(F32) for g in unpack_shards(grads, parts)) + (vector,)

    tokens_all = count * parts * copies
    outputs = [out[:count], pg[:count]]
    for member in range(5):
        grad_sum = total_grads[member]
        rate = RATES[member] / tokens_all**0.5
        moment_new = MOMENTUM * moments[member] + grad_sum
        weight_new = masters[member] - rate * (grad_sum + MOMENTUM * moment_new)
        average_new = AVERAGE * averages[member] + (1.0 - AVERAGE) * weight_new
        outputs.extend([grad_sum, moment_new, weight_new, average_new, weight_new.astype(BF)])
    return tuple(outputs)


def solution(mesh):
    tokens = P(("fsdp", "rep"), None)
    split, split_vector = P("fsdp", None), P(None, "fsdp")
    in_specs = (tokens, P(("fsdp", "rep")), tokens) + (split,) * 12 + (split_vector,) * 3
    out_specs = (tokens,) * 2 + (split,) * 20 + (split_vector,) * 5
    return jax.shard_map(on_device, mesh=mesh, in_specs=in_specs, out_specs=out_specs, check_vma=False)
```

time: 1120 us -> 552 us (0.49)
  matrix products: 370 us -> 0 us
  waiting for transfers between devices: 550 us -> 228 us
  Pallas kernels: 0 us -> 149 us
  other arithmetic: 67 us -> 27.9 us
  blocking collectives: 38.6 us -> 72.7 us
    dot_general x96 -> x0, matrix products: 370 us -> none  [the longest x24 83 us: masked_scores(): jnp.einsum('qd,kd->qk', query, keys, preferred_element_type=jnp.float32)]
    reduce_scatter x4 -> x1, waiting for transfers between devices: 412 us -> 161 us  [on_device(): lax.psum_scatter(grads, ('fsdp', 'rep'), scatter_dimension=0, tiled=True)]
    pallas_call x0 -> x5, Pallas kernels: none -> 149 us  [the longest x3 93.4 us: vmem_call(): pl.pallas_call(kernel, out_shape=[jax.ShapeDtypeStruct(s, d) for s, d in...]
    unnamed x11 -> x3, waiting for transfers between devices: 51.6 us -> 0.05 us
    psum x1 -> x0, waiting for transfers between devices: 40.3 us -> none  [on_device(): lax.psum(shard_grads[0].astype(jnp.bfloat16), 'rep').astype(jnp.float32)]
    psum x1, blocking collectives: 6.25 us -> 40.1 us  [on_device(): lax.psum(vector, ('fsdp', 'rep'))]
    convert_element_type x28 -> x10, other arithmetic: 39 us -> 11.3 us  [the longest x5 8.7 us: on_device(): weight_new.astype(BF)]
    all_gather x4 -> x2, waiting for transfers between devices: 46.2 us -> 66.9 us  [the longest x1 66.9 us: on_device(): full = lax.all_gather(quarter, ('fsdp', 'rep'), axis=0, tiled=True)]
  transfers between devices with their start and end apart: 10 -> 3, of which waited for: 7 -> 2; matrix products, arithmetic and copies ran while one was open for 39% -> 3% of each run, Pallas kernels for 0% -> 0%
where the time goes in v1:
time: 552 us; the launch traced here: 546 us
  waiting for transfers between devices  228 us (41%)
  Pallas kernels  149 us (27%)
  blocking collectives  72.7 us (13%)
  local copies, waits for them, and re-layouts  54 us (10%)
  other arithmetic  27.9 us (5%)
  between operations  14.4 us (3%)
    reduce_scatter x1, waiting for transfers between devices, on_device(): lax.psum_scatter(grads, ('fsdp', 'rep'), scatter_dimension=0, tiled=True)  161 us
    pallas_call x3, Pallas kernels, vmem_call(): pl.pallas_call(kernel, out_shape=[jax.ShapeDtypeStruct(s, d) for s, d in...  93.4 us
    all_gather x1, waiting for transfers between devices, on_device(): full = lax.all_gather(quarter, ('fsdp', 'rep'), axis=0, tiled=True)  66.9 us
    psum x1, blocking collectives, on_device(): lax.psum(vector, ('fsdp', 'rep'))  40.1 us
    pallas_call x1, Pallas kernels, attend_back(): pl.pallas_call(bwd_kernel, out_shape=jax.ShapeDtypeStruct(t.shape, BF), i...  36.8 us
    all_gather x1, blocking collectives, on_device(): lax.all_gather(vector_weight.astype(BF), 'fsdp', axis=1, tiled=True)  32.6 us
    pallas_call x1, Pallas kernels, attend(): pl.pallas_call(fwd_kernel, out_shape=jax.ShapeDtypeStruct((t.shape[0], D)...  18.8 us
    slice x2, local copies, waits for them, and re-layouts, on_device(): full[8:12]  11.7 us
  transfers between devices with their start and end apart: 3, of which 2 were waited for; matrix products, arithmetic and copies ran while one was open for 3% of the time, Pallas kernels for 0%

profile of v1, /device:TPU:0, one launch (start us, length us, event | category | flops | bytes accessed | tf_op | source)
XLA Modules:
  0.0 546.2 jit_solution(11971824872517635559)
XLA Ops:
  14.8 32.6 %all-gather = bf16[8,96,10]{1,2,0:T(8,128)(2,1)S(1)} all-gather(bf16[1,96,10]{1,2,0:T(8,128)(2,1)S(1)} %convert_bitcast_fusion.1), channel_id=1, replica_groups=mesh['fsdp'=8,'rep'=4] {'fsdp'}, dimensions={0}, use_global_device_ids=true | all-gather | bytes 17280 | tf_op jit(solution)/shard_map/all_gather | solution.py:390
  47.9 1.7 broadcast_select_fusion
  53.9 66.9 %all-gather.4.cloned.1.call-done = bf16[9216,768]{1,0:T(8,128)(2,1)} async-done(((bf16[288,768]{1,0:T(8,128)(2,1)}), bf16[9216,768]{1,0:T(8,128)(2,1)}) %all-gather.4.cloned.1.call-update) | async-done | bytes 14155792 | tf_op jit(solution)/shard_map/all_gather | solution.py:388
  120.8 2.4 slice.89
  123.2 2.2 slice.88
  125.4 6.8 %fusion.5 = (bf16[4,8,96,768]{3,2,0,1:T(8,128)(2,1)}, bf16[4,8,96,768]{3,2,0,1:T(8,128)(2,1)S(1)}) fusion(bf16[12,8,96,768]{3,2,0,1:T(8,128)(2,1)} %bitcast.46), kind=kLoop, calls=%fused_computation.34 | loop fusion | bytes 18874368 | tf_op jit(solution)/shard_map/slice | solution.py:400
  132.2 4.9 copy.81
  137.2 2.1 copy.79
  139.2 2.5 copy.80
  141.7 12.4 %project_in.1 = (bf16[1200,2304]{1,0:T(8,128)(2,1)}, bf16[1200,768]{1,0:T(8,128)(2,1)}) custom-call(bf16[1200,768]{1,0:T(8,128)(2,1)} %pad.7.x_ref, f32[16,768]{1,0:T(8,128)} %maximum_maximum_fusion.vec, bf16[3,768,768]{2,1,0:T(8,128)(2,1)} %bitcast.40), custom_call_target="tpu_custom_call" | custom-call | tf_op jit(solution)/shard_map/project_in/pallas_call | solution.py:316
  154.0 18.8 %attention_forward.1.o_ref = bf16[1200,768]{1,0:T(8,128)(2,1)S(1)} custom-call(s32[24]{0:T(128)S(1)} %copy-done.2, bf16[1200,2304]{1,0:T(8,128)(2,1)} %get-tuple-element.40.t_ref), custom_call_target="tpu_custom_call" | custom-call | tf_op jit(solution)/shard_map/attention_forward/pallas_call | solution.py:126
  174.1 62.2 %feed_forward.1 = (bf16[1200,768]{1,0:T(8,128)(2,1)}, f32[1200,768]{1,0:T(8,128)}, bf16[1200,768]{1,0:T(8,128)(2,1)}, bf16[768,768]{1,0:T(8,128)(2,1)}, bf16[4,7...) custom-call(bf16[1200,768]{1,0:T(8,128)(2,1)} %pad.7.x_ref, ...), custom_call_target="tpu_custom_call" | custom-call | tf_op jit(solution)/shard_map/feed_forward/pallas_call | solution.py:316
  237.8 36.8 %attention_backward.1.dt_ref = bf16[1200,2304]{1,0:T(8,128)(2,1)} custom-call(s32[24]{0:T(128)S(1)} %copy-done.2, bf16[1200,2304]{1,0:T(8,128)(2,1)} %get-tuple-element.40.t_ref, bf16[1200,768]{1,0:T(8,128)(2,1)S(1)} %copy-done.1), custom_call_target="tpu_custom_call" | custom-call | tf_op jit(solution)/shard_map/attention_backward/pallas_call | solution.py:132
  274.6 18.8 %project_in_back.1 = (f32[1200,768]{1,0:T(8,128)}, bf16[3,768,768]{2,1,0:T(8,128)(2,1)}, f32[8,768]{1,0:T(8,128)}) custom-call(bf16[1200,768]{1,0:T(8,128)(2,1)} %pad.7.x_ref, bf16[1200,768]{1,0:T(8,128)(2,1)} %get-tuple-element.42.a1_ref, bf16[1200,2304]{1,0:T(8,128)(2,1)} %attention_backward.1.dt_ref, f32[1200,768]{1,0:T(8,128)} %get-tuple-element.44.dm_ref, ...), custom_call_target="tpu_custom_call" | custom-call | tf_op jit(solution)/shard_map/project_in_back/pallas_call | solution.py:316
  293.4 7.2 %maximum_bitcast_fusion = bf16[8,12,96,768]{3,2,0,1:T(8,128)(2,1)S(1)} fusion(bf16[4,8,96,768]{3,2,1,0:T(8,128)(2,1)} %bitcast.50, bf16[4,8,96,768]{3,2,1,0:T(8,128)(2,1)} %bitcast.49, bf16[1,8,96,768]{3,2,1,0:T(8,128)(2,1)S(1)} %bitcast.60, bf16[3,8,96,768]{3,2,1,0:T(8,128)(2,1)} %bitcast.52), kind=kLoop, calls=%fused_computation | loop fusion | flops 21233664 | bytes 28311552 | tf_op jit(solution)/shard_map/transpose | solution.py:405
  300.6 5.6 %copy.82 = bf16[8,12,96,768]{3,2,1,0:T(8,128)(2,1)} copy(bf16[8,12,96,768]{3,2,0,1:T(8,128)(2,1)S(1)} %maximum_bitcast_fusion) | data formatting | bytes 28311552 | tf_op jit(solution)/shard_map/transpose | solution.py:405
  306.3 161.1 %reduce-scatter.2.cloned.1.call-done = bf16[288,768]{1,0:T(8,128)(2,1)} async-done(((bf16[9216,768]{1,0:T(8,128)(2,1)}), bf16[288,768]{1,0:T(8,128)(2,1)}) %reduce-scatter.2.cloned.1.call-update) | async-done | bytes 442384 | tf_op jit(solution)/shard_map/reduce_scatter | solution.py:406
  468.8 4.1 slice.76
  474.9 40.1 %psum.7 = f32[10,768]{1,0:T(8,128)S(1)} all-reduce(f32[10,768]{1,0:T(8,128)S(1)} %concatenate.28), channel_id=1, replica_groups=mesh['fsdp'=8,'rep'=4] {'fsdp','rep'}, use_global_device_ids=true, to_apply=%region_1.2 | all-reduce | flops 7680 | bytes 61440 | tf_op jit(solution)/shard_map/psum | solution.py:412
  521.7 1.6 reshape.132
  523.4 2.2 fusion.3
  525.6 1.8 add_multiply_fusion.3
  531.0 3.0 fusion.1
  536.5 1.6 fusion.2
  (117 shorter events, 32.5 us)
Async XLA Ops:
  7.2 113.6 %all-gather.4.cloned.1.call-start = ((), (), s32[]{:S(2)}) async-start(), calls=%async_computation.1 | async-start | bytes 14598144 | tf_op jit(solution)/shard_map/all_gather | solution.py:388
  8.2 2.3 copy-start.7
  13.7 33.8 %copy-start.2 = (s32[24]{0:T(128)S(1)}, s32[24]{0:T(128)}, u32[]{:S(2)}) copy-start(s32[24]{0:T(128)} %clips.3) | copy-start | bytes 292
  14.7 452.7 %reduce-scatter.2.cloned.1.call-start = ((), (), s32[]{:S(2)}) async-start(), calls=%async_computation.2 | async-start | bytes 14598144 | tf_op jit(solution)/shard_map/reduce_scatter | solution.py:406
  49.6 2.2 copy-start.13
  274.6 18.8 %copy-start.16 = (bf16[768,768]{1,0:T(8,128)(2,1)S(1)}, bf16[768,768]{1,0:T(8,128)(2,1)}, u32[]{:S(2)}) copy-start(bf16[768,768]{1,0:T(8,128)(2,1)} %get-tuple-element.47) | copy-start | bytes 3538948
  306.2 161.2 %copy-start.14 = (bf16[1200,768]{1,0:T(8,128)(2,1)S(1)}, bf16[1200,768]{1,0:T(8,128)(2,1)}, u32[]{:S(2)}) copy-start(bf16[1200,768]{1,0:T(8,128)(2,1)} %get-tuple-element.41) | copy-start | bytes 5529604
  306.2 210.1 %all-gather.6.cloned.1.call-start = ((), (), s32[]{:S(2)}) async-start(), calls=%async_computation.3 | async-start | bytes 2211840 | tf_op jit(solution)/shard_map/all_gather | solution.py:407
  468.8 4.8 copy-start.30
  468.8 46.3 %copy-start.29 = (f32[10,96]{1,0:T(8,128)S(1)}, f32[10,96]{1,0:T(8,128)}, u32[]{:S(2)}) copy-start(f32[10,96]{1,0:T(8,128)} %param.34) | copy-start | bytes 11524
  468.8 47.0 %copy-start.28 = (f32[10,96]{1,0:T(8,128)S(1)}, f32[10,96]{1,0:T(8,128)}, u32[]{:S(2)}) copy-start(f32[10,96]{1,0:T(8,128)} %param.35) | copy-start | bytes 11524
  515.7 3.1 copy-start.26
  521.7 1.7 copy-start.22
  523.4 11.8 %copy-start.9 = (f32[96,3072]{1,0:T(8,128)}, f32[96,3072]{1,0:T(8,128)S(1)}, u32[]{:S(2)}) copy-start(f32[96,3072]{1,0:T(8,128)S(1)} %reshape.132) | copy-start | bytes 3538948
  523.4 4.0 copy-start.10
  523.4 4.0 copy-start.11
  523.4 4.0 copy-start.23
  525.6 3.1 copy-start.21
  528.7 5.3 copy-start.12
  528.7 1.9 copy-start.6
  528.7 2.3 copy-start.17
  531.0 3.0 copy-start.18
  534.0 2.1 copy-start.8
  534.0 2.5 copy-start.19
  (10 other events, 13.5 us)
Sparse Core Ops, SparseCore 0:
  14.8 105.9 all-gather.3
  306.4 160.9 reduce-scatter.1
  468.9 20.0 all-gather.5

commit v2 on v1

--- a/solution.py
+++ b/solution.py
@@ -44,10 +44,14 @@
     tail = slots*SLOT//16*16
     ref[pl.ds(tail, ref.shape[0]-tail), :] = jnp.zeros((ref.shape[0]-tail, ref.shape[1]), BF)
 
-def fwd_kernel(clips, t_ref, o_ref, bias):
+def fwd_kernel(clips, t_ref, g_ref, o_ref, dy_ref, bias):
     slots = clips.shape[0]
     rows = t_ref.shape[0]; D = o_ref.shape[1]
     clear_tail(o_ref, slots)
+    clear_tail(dy_ref, slots)
+    slot = (lax.broadcasted_iota(jnp.int32,(slots*SLOT,1),0)*1338) >> 16
+    live = lax.fori_loop(0, slots, lambda s, was: jnp.where((slot == s) & (clips[s] >= 0), 1.0, was), jnp.zeros((slots*SLOT,1),F32), unroll=True)
+    dy_ref[pl.ds(0,slots*SLOT), :] = jnp.where(live > 0, g_ref[...].astype(F32), 0.0).astype(BF)
     def group(g, start):
         @pl.when(start < slots)
         def _():
@@ -121,13 +125,13 @@
         return jnp.where(start < slots, group_end(clips, start, slots), start)
     lax.fori_loop(0, (2*slots)//(LIVE_MAX+1)+1, group, 0)
 
-def attend(clips, t):
+def attend(clips, t, g):
     D=t.shape[1]//3
-    return pl.pallas_call(fwd_kernel, out_shape=jax.ShapeDtypeStruct((t.shape[0],D),BF),
-      in_specs=[pl.BlockSpec(memory_space=pltpu.SMEM), pl.BlockSpec(memory_space=pltpu.VMEM)],
-      out_specs=pl.BlockSpec(memory_space=pltpu.VMEM),
+    return pl.pallas_call(fwd_kernel, out_shape=[jax.ShapeDtypeStruct((t.shape[0],D),BF)]*2,
+      in_specs=[pl.BlockSpec(memory_space=pltpu.SMEM)]+[pl.BlockSpec(memory_space=pltpu.VMEM)]*2,
+      out_specs=[pl.BlockSpec(memory_space=pltpu.VMEM)]*2,
       scratch_shapes=[pltpu.VMEM((WIN,WIN),F32)],
-      compiler_params=pltpu.CompilerParams(vmem_limit_bytes=48*2**20),name="attention_forward")(clips,t)
+      compiler_params=pltpu.CompilerParams(vmem_limit_bytes=48*2**20),name="attention_forward")(clips,t,g)
 def attend_back(clips, t, do):
     return pl.pallas_call(bwd_kernel, out_shape=jax.ShapeDtypeStruct(t.shape,BF),
       in_specs=[pl.BlockSpec(memory_space=pltpu.SMEM)]+[pl.BlockSpec(memory_space=pltpu.VMEM)]*2,
@@ -198,9 +202,10 @@
 
 def qkv_block(a1_ref, w_ref, t_ref, part):
     width = a1_ref.shape[1]
+    weight = w_ref[part].reshape(width, width)
 
     def one(win):
-        out = dot_nn(a1_ref[win, :], w_ref[...])
+        out = dot_nn(a1_ref[win, :], weight)
         if part == 0:
             out = out * HEAD_DIM**-0.5
         t_ref[win, pl.ds(part * width, width)] = out.astype(BF)
@@ -211,7 +216,7 @@
 def qkv_kernel(x_ref, vec, w_ref, t_ref, a1_ref):
     qkv_norm(x_ref, vec, a1_ref)
     for part in range(3):
-        qkv_block(a1_ref, w_ref.at[part], t_ref, part)
+        qkv_block(a1_ref, w_ref, t_ref, part)
 
 
 def middle_step(x_ref, o_ref, vec, wo_ref, m_ref, a2_ref):
@@ -324,6 +329,487 @@
     )(*ins)
 
 
+MESH = pl.DeviceIdType.MESH
+
+
+class Place:
+    def __init__(self, parts, sh, width):
+        mine, copy = lax.axis_index("fsdp"), lax.axis_index("rep")
+        self.outer_count = parts // 2
+        self.outer, self.inner = mine // 2, mine % 2
+        self.plane, self.core = copy // 2, copy % 2
+        self.third = sh // 3
+        self.half = width // 2
+
+    def device(self, outer=None, inner=None, plane=None, core=None):
+        outer = self.outer if outer is None else outer
+        inner = self.inner if inner is None else inner
+        plane = self.plane if plane is None else plane
+        core = self.core if core is None else core
+        return (outer * 2 + inner, plane * 2 + core)
+
+    def far(self, k):
+        return (self.outer + k) % self.outer_count
+
+    def ranks(self):
+        return range(1, self.outer_count)
+
+    def columns(self, core=None):
+        core = self.core if core is None else core
+        return pl.ds(pl.multiple_of(core * self.half, 128), self.half)
+
+    def held(self):
+        return pl.ds(pl.multiple_of(self.plane * self.third, 16), 2 * self.third)
+
+    def own(self, plane=None):
+        plane = self.plane if plane is None else plane
+        return pl.ds(pl.multiple_of(plane * (2 * self.third), 16), self.third)
+
+    def peers(self):
+        return [self.device(outer=self.far(k)) for k in self.ranks()] + [
+            self.device(inner=1 - self.inner),
+            self.device(plane=1 - self.plane),
+            self.device(core=1 - self.core),
+        ]
+
+    def greet(self):
+        barrier = pltpu.get_barrier_semaphore()
+        peers = self.peers()
+        for peer in peers:
+            pl.semaphore_signal(barrier, inc=1, device_id=peer, device_id_type=MESH)
+        pl.semaphore_wait(barrier, len(peers))
+
+
+def remote(src, dst, sems, index, device):
+    return pltpu.make_async_remote_copy(
+        src_ref=src, dst_ref=dst, send_sem=sems[0].at[index], recv_sem=sems[1].at[index],
+        device_id=device, device_id_type=MESH,
+    )
+
+
+def start(copies):
+    for copy in copies:
+        copy.start()
+
+
+def landed(copies):
+    for copy in copies:
+        copy.wait_recv()
+
+
+def sent(copies):
+    for copy in copies:
+        copy.wait_send()
+
+
+class Gather:
+    def __init__(self, place, shard, full, sems):
+        self.p, self.shard, self.full, self.sems = place, shard, full, sems
+
+    def far(self, b):
+        p = self.p
+        return [
+            remote(
+                self.shard.at[b, p.held(), p.columns()],
+                self.full.at[b, p.outer, p.inner, p.held(), p.columns()],
+                self.sems, (b, k - 1), p.device(outer=p.far(k)),
+            )
+            for k in p.ranks()
+        ]
+
+    def pair(self, b, which):
+        p = self.p
+        if which == 0:
+            ref = self.full.at[b, :, p.inner, p.held(), p.columns()]
+            device = p.device(inner=1 - p.inner)
+        elif which == 1:
+            ref = self.full.at[b, :, :, p.own(), p.columns()]
+            device = p.device(plane=1 - p.plane)
+        else:
+            ref = self.full.at[b, :, :, :, p.columns()]
+            device = p.device(core=1 - p.core)
+        return [remote(ref, ref, self.sems, (b, p.outer_count - 1 + which), device)]
+
+    def put_own(self, b):
+        p = self.p
+        self.full[b, p.outer, p.inner, p.held(), p.columns()] = self.shard[b, p.held(), p.columns()]
+
+    def step(self, s, count, lag):
+        for stage in range(5):
+            @pl.when((s >= stage * lag) & (s < count + stage * lag))
+            def _():
+                b = s - stage * lag
+                if stage == 0:
+                    start(self.far(b))
+                    self.put_own(b)
+                else:
+                    landed(self.far(b) if stage == 1 else self.pair(b, stage - 2))
+                    if stage < 4:
+                        start(self.pair(b, stage - 1))
+
+    def finish(self, count):
+        @pl.loop(0, count)
+        def _(b):
+            sent(self.far(b))
+            for which in range(3):
+                sent(self.pair(b, which))
+
+
+def gather_sems(blocks, parts):
+    shape = (blocks, parts // 2 - 1 + 3)
+    return [pltpu.SemaphoreType.DMA(shape), pltpu.SemaphoreType.DMA(shape)]
+
+
+class Reduce:
+    def __init__(self, place, grad, out, bufs, sems):
+        self.p, self.grad, self.out, self.sems = place, grad, out, sems
+        self.from_core, self.from_plane, self.from_inner, self.from_far, self.part, self.from_part = bufs
+
+    @staticmethod
+    def scratch(blocks, parts, sh, width):
+        outer, third, half = parts // 2, sh // 3, width // 2
+        shape = (blocks, outer - 1 + 5)
+        return [
+            pltpu.VMEM((blocks, outer, 2, sh, half), BF),
+            pltpu.VMEM((blocks, outer, 2, third, half), BF),
+            pltpu.VMEM((blocks, outer, 2 * third, half), BF),
+            pltpu.VMEM((blocks, outer - 1, 2 * third, half), BF),
+            pltpu.VMEM((blocks, 2 * third, half), BF),
+            pltpu.VMEM((blocks, 2 * third, half), BF),
+            pltpu.SemaphoreType.DMA(shape),
+            pltpu.SemaphoreType.DMA(shape),
+        ]
+
+    def copies(self, b, stage):
+        p = self.p
+        base = p.outer_count - 1
+        if stage == 0:
+            src, dst = self.grad.at[b, :, :, :, p.columns(1 - p.core)], self.from_core.at[b]
+            device = p.device(core=1 - p.core)
+        elif stage == 1:
+            src, dst = self.grad.at[b, :, :, p.own(1 - p.plane), p.columns()], self.from_plane.at[b]
+            device = p.device(plane=1 - p.plane)
+        elif stage == 2:
+            src, dst = self.grad.at[b, :, 1 - p.inner, p.held(), p.columns()], self.from_inner.at[b]
+            device = p.device(inner=1 - p.inner)
+        elif stage == 3:
+            return [
+                remote(
+                    self.grad.at[b, p.far(k), p.inner, p.held(), p.columns()],
+                    self.from_far.at[b, k - 1], self.sems, (b, k - 1), p.device(outer=p.far(k)),
+                )
+                for k in p.ranks()
+            ]
+        elif stage == 4:
+            src, dst = self.part.at[b], self.from_part.at[b]
+            device = p.device(plane=1 - p.plane)
+        else:
+            src = dst = self.out.at[b, :, p.columns()]
+            device = p.device(core=1 - p.core)
+        return [remote(src, dst, self.sems, (b, base + (stage if stage < 3 else stage - 1)), device)]
+
+    def add(self, b, stage):
+        p = self.p
+        if stage == 0:
+            @pl.loop(0, p.outer_count)
+            def _(o):
+                for i in range(2):
+                    index = (b, o, i, slice(None), p.columns())
+                    self.grad[index] = (self.grad[index].astype(F32) + self.from_core[b, o, i].astype(F32)).astype(BF)
+        elif stage == 1:
+            for i in range(2):
+                @pl.loop(0, p.outer_count)
+                def _(o):
+                    index = (b, o, i, p.own(), p.columns())
+                    self.grad[index] = (self.grad[index].astype(F32) + self.from_plane[b, o, i].astype(F32)).astype(BF)
+        elif stage == 2:
+            @pl.loop(0, p.outer_count)
+            def _(o):
+                index = (b, o, p.inner, p.held(), p.columns())
+                self.grad[index] = (self.grad[index].astype(F32) + self.from_inner[b, o].astype(F32)).astype(BF)
+        elif stage == 3:
+            total = self.grad[b, p.outer, p.inner, p.held(), p.columns()].astype(F32)
+            for k in p.ranks():
+                total += self.from_far[b, k - 1].astype(F32)
+            self.part[b] = total.astype(BF)
+        elif stage == 4:
+            third = p.third
+            for plane in range(2):
+                @pl.when(p.plane == plane)
+                def _():
+                    mine, other = self.part, self.from_part
+                    first, last = (mine, other) if plane == 0 else (other, mine)
+                    self.out[b, pl.ds(0, third), p.columns()] = first[b, pl.ds(0, third), :]
+                    middle = first[b, pl.ds(third, third), :].astype(F32) + last[b, pl.ds(0, third), :].astype(F32)
+                    self.out[b, pl.ds(third, third), p.columns()] = middle.astype(BF)
+                    self.out[b, pl.ds(2 * third, third), p.columns()] = last[b, pl.ds(third, third), :]
+
+    def stage(self, b, stage):
+        if stage > 0:
+            landed(self.copies(b, stage - 1))
+            self.add(b, stage - 1)
+        if stage < 6:
+            start(self.copies(b, stage))
+
+    def step(self, s, count, lag):
+        for stage in range(7):
+            @pl.when((s >= stage * lag) & (s < count + stage * lag))
+            def _():
+                self.stage(s - stage * lag, stage)
+
+    def finish(self, count):
+        @pl.loop(0, count)
+        def _(b):
+            for stage in range(6):
+                sent(self.copies(b, stage))
+
+
+class Vector:
+    def __init__(self, place, total, bufs, sems, everywhere):
+        self.p, self.total, self.sems = place, total, sems
+        self.pairs, self.fars = bufs
+        self.order = (0, 1, 2) if everywhere else (2,)
+
+    @staticmethod
+    def scratch(parts, shape, dtype):
+        sems = (parts // 2 - 1 + 3,)
+        return [
+            pltpu.VMEM((6,) + shape, dtype), pltpu.VMEM((parts // 2,) + shape, dtype),
+            pltpu.SemaphoreType.DMA(sems), pltpu.SemaphoreType.DMA(sems),
+        ]
+
+    def pair(self, which):
+        p = self.p
+        device = (
+            p.device(core=1 - p.core), p.device(plane=1 - p.plane), p.device(inner=1 - p.inner)
+        )[which]
+        return [remote(self.pairs.at[2 * which], self.pairs.at[2 * which + 1], self.sems, p.outer_count - 1 + which, device)]
+
+    def far(self):
+        p = self.p
+        mine = self.fars.at[p.outer]
+        return [remote(mine, mine, self.sems, k - 1, p.device(outer=p.far(k))) for k in p.ranks()]
+
+    def far_landed(self):
+        p = self.p
+        for k in p.ranks():
+            theirs = self.fars.at[(p.outer + p.outer_count - k) % p.outer_count]
+            remote(theirs, theirs, self.sems, k - 1, p.device(outer=p.far(k))).wait_recv()
+
+    def stage(self, number):
+        order = self.order
+        if number > 0 and number <= len(order):
+            which = order[number - 1]
+            landed(self.pair(which))
+            self.total[...] = self.total[...] + self.pairs[2 * which + 1]
+        if number < len(order):
+            which = order[number]
+            self.pairs[2 * which] = self.total[...]
+            start(self.pair(which))
+        elif number == len(order):
+            self.fars[self.p.outer] = self.total[...]
+            start(self.far())
+        else:
+            self.far_landed()
+            total = self.fars[0]
+            for o in range(1, self.p.outer_count):
+                total = total + self.fars[o]
+            self.total[...] = total
+
+    def stages(self):
+        return len(self.order) + 2
+
+    def finish(self):
+        for which in self.order:
+            sent(self.pair(which))
+        sent(self.far())
+
+
+FIRST_BLOCKS = 6
+TILES = 3
+
+
+def flat(ref, b):
+    block = ref[b]
+    return block.reshape(block.shape[0] * block.shape[1] * block.shape[2], block.shape[3])
+
+
+def gather_kernel(parts, x_ref, vec_in, shard, t_ref, a1_ref, xp_ref, full, vec, *scratch):
+    count, width = x_ref.shape
+    rows = xp_ref.shape[0]
+    place = Place(parts, shard.shape[1], width)
+    weights = Gather(place, shard, full, scratch[0:2])
+    vectors = Vector(place, vec, scratch[2:4], scratch[4:6], False)
+    place.greet()
+    weights.step(0, FIRST_BLOCKS, 1)
+    vec[...] = vec_in[...]
+    vectors.stage(0)
+    tail = count // 16 * 16
+    xp_ref[pl.ds(tail, rows - tail), :] = jnp.zeros((rows - tail, width), BF)
+    xp_ref[pl.ds(0, count), :] = x_ref[...]
+    vectors.stage(1)
+    weights.step(1, FIRST_BLOCKS, 1)
+    vectors.stage(2)
+    weights.step(2, FIRST_BLOCKS, 1)
+    qkv_norm(xp_ref, vec, a1_ref)
+    weights.step(3, FIRST_BLOCKS, 1)
+    for s in range(4, FIRST_BLOCKS + 4):
+        weights.step(s, FIRST_BLOCKS, 1)
+        if s - 4 < 3:
+            qkv_block(a1_ref, full, t_ref, s - 4)
+    weights.finish(FIRST_BLOCKS)
+    vectors.finish()
+
+
+def feed_comm_kernel(
+    parts, x_ref, o_ref, dy_ref, vec, wo_ref, we0_ref, wc0_ref, shard,
+    out_ref, dm_ref, do_ref, dz_ref, grad_out, sums, be_ref,
+    a2_ref, y_ref, da2_ref, full, grad, local, *scratch,
+):
+    rows, width = x_ref.shape
+    sh = shard.shape[1]
+    place = Place(parts, sh, width)
+    later = shard.shape[0]
+    weights = Gather(place, shard, full.at[pl.ds(2, later)], scratch[0:2])
+    grads = Reduce(place, grad, grad_out, scratch[2:8], scratch[8:10])
+    place.greet()
+    du_ref, h_ref = do_ref, dz_ref
+    ready = [
+        pltpu.make_async_copy(ref.at[0], full.at[b], local.at[b]) for b, ref in enumerate((we0_ref, wc0_ref))
+    ]
+    start(ready)
+
+    def win(i):
+        return pl.ds(i * RT, RT)
+
+    wo = flat(wo_ref, 0)
+    weights.step(0, later, 1)
+    for i in range(TILES):
+        middle = x_ref[win(i), :].astype(F32) + (dot_nn(o_ref[win(i), :], wo) + vec[2:3, :])
+        dm_ref[win(i), :] = middle
+        unit, _ = norm_parts(middle)
+        a2_ref[win(i), :] = (unit * vec[3:4, :] + vec[4:5, :]).astype(BF)
+        y_ref[win(i), :] = jnp.zeros((RT, width), F32)
+        da2_ref[win(i), :] = jnp.zeros((RT, width), F32)
+        weights.step(i + 1, later, 1)
+    for copy in ready:
+        copy.wait()
+
+    def passing(j, i):
+        for parity in range(2):
+            for back in range(3):
+                stage = i - 3 - parity + 5 * back
+                if 0 <= stage <= 6:
+                    if back == 0:
+                        grads.stage(2 * j + parity, stage)
+                    else:
+                        @pl.when(j >= back)
+                        def _():
+                            grads.stage(2 * (j - back) + parity, stage)
+
+    @pl.loop(0, 4)
+    def _(j):
+        bias = vec[pl.ds(6 + j, 1), :]
+        be_sum = jnp.zeros((1, width), F32)
+        for i in range(TILES):
+            hidden, slope = gelu_pair(dot_nn(a2_ref[win(i), :], flat(full, 2 * j)) + bias)
+            hidden = hidden.astype(BF)
+            h_ref[win(i), :] = hidden
+            du = (dot_nt(dy_ref[win(i), :], flat(full, 2 * j + 1)) * slope).astype(BF)
+            du_ref[win(i), :] = du
+            be_sum += column_sum(du.astype(F32))
+            y_ref[win(i), :] += dot_nn(hidden, flat(full, 2 * j + 1))
+            da2_ref[win(i), :] += dot_nt(du, flat(full, 2 * j))
+            weights.step(4 + 5 * j + i, later, 1)
+            passing(j, i)
+        be_ref[pl.ds(j, 1), :] = be_sum
+        grad[2 * j] = dot_tn(h_ref[...], dy_ref[...]).astype(BF).reshape(grad.shape[1:])
+        weights.step(4 + 5 * j + 3, later, 1)
+        passing(j, 3)
+        grad[2 * j + 1] = dot_tn(a2_ref[...], du_ref[...]).astype(BF).reshape(grad.shape[1:])
+        weights.step(4 + 5 * j + 4, later, 1)
+        passing(j, 4)
+
+    sums[...] = jnp.zeros_like(sums)
+    for slot in range(5, 12):
+        i = slot - 5
+        if i < TILES:
+            middle = dm_ref[win(i), :]
+            out_ref[win(i), :] = (middle + (y_ref[win(i), :] + vec[5:6, :])).astype(BF)
+            unit, scale = norm_parts(middle)
+            da2 = da2_ref[win(i), :]
+            dy = dy_ref[win(i), :].astype(F32)
+            dm = dy + norm_back(da2, vec[3:4, :], unit, scale)
+            dm_ref[win(i), :] = dm
+            dz = dm.astype(BF)
+            dz_ref[win(i), :] = dz
+            do_ref[win(i), :] = dot_nt(dz, wo).astype(BF)
+            sums[0:1, :] += column_sum(da2 * unit)
+            sums[1:2, :] += column_sum(da2)
+            sums[2:3, :] += column_sum(dz.astype(F32))
+            sums[3:4, :] += column_sum(dy)
+        for j in range(2, 4):
+            for parity in range(2):
+                stage = slot - 3 - parity + 5 * (3 - j)
+                if 0 <= stage <= 6:
+                    grads.stage(2 * j + parity, stage)
+    weights.finish(later)
+    grads.finish(8)
+
+
+def first_comm_kernel(
+    parts, x_ref, a1_ref, o_ref, dz_ref, dt_ref, dm_ref, vec, wi_ref, sums_two, be_ref,
+    pg_ref, grad_out, total, grad, *scratch,
+):
+    rows, width = x_ref.shape
+    place = Place(parts, width // parts, width)
+    grads = Reduce(place, grad, grad_out, scratch[0:6], scratch[6:8])
+    vectors = Vector(place, total, scratch[8:10], scratch[10:12], True)
+    place.greet()
+    total[...] = jnp.zeros_like(total)
+    total[2:3, :] = sums_two[2:3, :]
+    total[3:5, :] = sums_two[0:2, :]
+    total[5:6, :] = sums_two[3:4, :]
+    total[6:10, :] = be_ref[0:4, :]
+    grad[0] = dot_tn(o_ref[...], dz_ref[...]).astype(BF).reshape(grad.shape[1:])
+    grads.step(0, 4, 1)
+    for part in range(3):
+        block = dot_tn(a1_ref[...], dt_ref[:, pl.ds(part * width, width)]).astype(BF)
+        grad[part + 1] = block.reshape(grad.shape[1:])
+        grads.step(part + 1, 4, 1)
+    for i in range(TILES):
+        win = pl.ds(i * RT, RT)
+        da1 = dot_nt(dt_ref[win, pl.ds(0, width)], flat(wi_ref, 0))
+        da1 += dot_nt(dt_ref[win, pl.ds(width, width)], flat(wi_ref, 1))
+        da1 += dot_nt(dt_ref[win, pl.ds(2 * width, width)], flat(wi_ref, 2))
+        unit, scale = norm_parts(x_ref[win, :].astype(F32))
+        pg_ref[win, :] = dm_ref[win, :] + norm_back(da1, vec[0:1, :], unit, scale)
+        total[0:1, :] += column_sum(da1 * unit)
+        total[1:2, :] += column_sum(da1)
+        grads.step(4 + i, 4, 1)
+    for s in range(7, 10):
+        vectors.stage(s - 7)
+        grads.step(s, 4, 1)
+    for number in range(3, vectors.stages()):
+        vectors.stage(number)
+    grads.finish(4)
+    vectors.finish()
+
+
+def comm_call(kernel, name, which, ins, outs, scratch, far=()):
+    return pl.pallas_call(
+        kernel,
+        out_shape=[jax.ShapeDtypeStruct(s, d) for s, d in outs],
+        in_specs=[pl.BlockSpec(memory_space=pl.ANY) if i in far else VM for i in range(len(ins))],
+        out_specs=[VM] * len(outs),
+        scratch_shapes=scratch,
+        compiler_params=pltpu.CompilerParams(
+            vmem_limit_bytes=62 * 2**20, collective_id=which, has_side_effects=True
+        ),
+        name=name,
+    )(*ins)
+
+
 def run_qkv(x, vec, wi):
     rows, width = x.shape
     return vmem_call(
@@ -363,6 +849,94 @@
     wi = blocks[0:3].swapaxes(0, 1).reshape(rows, 3 * width)
     we = blocks[4:8].reshape(4, rows, parts, rows).transpose(1, 2, 0, 3).reshape(rows, 4 * width)
     return wi, blocks[3], we, blocks[8:12].reshape(4 * rows, width)
+
+
+def plain_path(patches, slot_clip, out_grad, masters, vector_weight):
+    parts, copies = lax.axis_size("fsdp"), lax.axis_size("rep")
+    mine, copy = lax.axis_index("fsdp"), lax.axis_index("rep")
+    count, width = patches.shape
+    rows = (count + RT - 1) // RT * RT
+    sh = width // parts
+    packed = pack_shards(*(m.astype(BF) for m in masters), parts).reshape(12 * sh, width)
+    piece = 12 * sh // copies
+    quarter = lax.dynamic_slice_in_dim(packed, copy * piece, piece, 0)
+    full = lax.all_gather(quarter, ("fsdp", "rep"), axis=0, tiled=True)
+    full = full.reshape(parts, 12, sh, width).swapaxes(0, 1).reshape(12, width, width)
+    vec = lax.all_gather(vector_weight.astype(BF), "fsdp", axis=1, tiled=True).astype(F32)
+    be = vec[6:].reshape(parts, 4, sh).swapaxes(0, 1).reshape(4, width)
+    vec = jnp.concatenate([vec[:6], be, jnp.zeros((6, width), F32)], axis=0)
+
+    pad = ((0, rows - count), (0, 0))
+    x = jnp.pad(patches, pad)
+    t, a1 = run_qkv(x, vec, full[0:3])
+    o, dy = attend(slot_clip, t, out_grad)
+    out, dm, do, gwo, gwe, gwc, sums_two, sums_be = run_feed(x, o, dy, vec, full[3], full[4:8], full[8:12])
+    dt = attend_back(slot_clip, t, do)
+    pg, gwi, sums_one = run_first(x, a1, dt, dm, vec, full[0:3])
+
+    grads = jnp.concatenate([gwi, gwo[None], gwe, gwc], axis=0)
+    grads = grads.reshape(12, parts, sh, width).swapaxes(0, 1).reshape(parts * 12 * sh, width)
+    grads = lax.psum_scatter(grads, ("fsdp", "rep"), scatter_dimension=0, tiled=True)
+    grads = lax.all_gather(grads, "rep", axis=0, tiled=True).reshape(12, sh, width)
+    be_grad = sums_be[::8].reshape(4, parts, sh).swapaxes(0, 1).reshape(4, width)
+    vector = jnp.concatenate(
+        [sums_one[0:2], sums_two[2:3], sums_two[0:2], sums_two[3:4], be_grad], axis=0
+    )
+    vector = lax.dynamic_slice_in_dim(lax.psum(vector, ("fsdp", "rep")), mine * sh, sh, 1)
+    return out[:count], pg[:count], tuple(g.astype(F32) for g in unpack_shards(grads, parts)) + (vector,)
+
+
+def direct_path(patches, slot_clip, out_grad, masters, vector_weight):
+    parts = lax.axis_size("fsdp")
+    mine = lax.axis_index("fsdp")
+    count, width = patches.shape
+    rows = (count + RT - 1) // RT * RT
+    sh = width // parts
+    block = (parts // 2, 2, sh, width)
+    wide, low = ((rows, width), F32), ((rows, width), BF)
+
+    packed = pack_shards(*(m.astype(BF) for m in masters), parts)
+    first = jnp.concatenate([packed[0:5], packed[8:9]], axis=0)
+    later = packed[5:8], packed[9:12]
+    later = jnp.stack(later, axis=1).reshape(6, sh, width)
+    vector_low = vector_weight.astype(BF).astype(F32)
+    place = jnp.arange(parts)[None, :, None]
+    row = jnp.arange(4)[:, None, None]
+    apart = parts // 4
+    top = jnp.where(place == mine, vector_low[:6, None, :], 0.0)
+    be = jnp.repeat(vector_low[6:], apart, axis=0)[None]
+    be = jnp.where((row == mine % 4) & (place % apart == mine // 4), be, 0.0)
+    placed = jnp.concatenate([top, be, jnp.zeros((6, parts, sh), F32)], axis=0).reshape(16, width)
+
+    t, a1, x, full, vec = comm_call(
+        functools.partial(gather_kernel, parts), "gather_project_in", 0, (patches, placed, first),
+        [((rows, 3 * width), BF), low, low, ((FIRST_BLOCKS,) + block, BF), ((16, width), F32)],
+        gather_sems(FIRST_BLOCKS, parts) + Vector.scratch(parts, (16, width), F32),
+    )
+    o, dy = attend(slot_clip, t, out_grad)
+    out, dm, do, dz, grads_two, sums_two, sums_be = comm_call(
+        functools.partial(feed_comm_kernel, parts), "feed_forward_reduce", 1,
+        (x, o, dy, vec, full[3:4], full[4:5], full[5:6], later),
+        [low, wide, low, low, ((8, sh, width), BF), ((8, width), F32), ((8, width), F32)],
+        [pltpu.VMEM(*low), pltpu.VMEM(*wide), pltpu.VMEM(*wide),
+         pltpu.VMEM((8,) + block, BF), pltpu.VMEM((8,) + block, BF), pltpu.SemaphoreType.DMA((2,))]
+        + gather_sems(6, parts) + Reduce.scratch(8, parts, sh, width), far=(5, 6),
+    )
+    dt = attend_back(slot_clip, t, do)
+    pg, grads_one, vector = comm_call(
+        functools.partial(first_comm_kernel, parts), "project_in_back_reduce", 2,
+        (x, a1, o, dz, dt, dm, vec, full[0:3], sums_two, sums_be),
+        [wide, ((4, sh, width), BF), ((16, width), F32)],
+        [pltpu.VMEM((4,) + block, BF)] + Reduce.scratch(4, parts, sh, width)
+        + Vector.scratch(parts, (16, width), F32),
+    )
+    blocks = jnp.concatenate([grads_one[1:4], grads_one[0:1], grads_two[1::2], grads_two[0::2]], axis=0)
+    top = lax.dynamic_slice_in_dim(vector[:6], mine * sh, sh, 1)
+    be = lax.dynamic_slice_in_dim(vector, 6 + mine % 4, 1, 0).reshape(4, apart, sh)
+    be = lax.dynamic_index_in_dim(be, mine // 4, 1, keepdims=False)
+    vector = jnp.concatenate([top, be], axis=0)
+    grads = tuple(g.astype(F32) for g in unpack_shards(blocks, parts)) + (vector,)
+    return out[:count], pg[:count], grads
 
 
 def on_device(
@@ -377,43 +951,13 @@
     moments = (project_in_moment, project_out_moment, expand_moment, contract_moment, vector_moment)
     averages = (project_in_average, project_out_average, expand_average, contract_average, vector_average)
     parts, copies = lax.axis_size("fsdp"), lax.axis_size("rep")
-    mine, copy = lax.axis_index("fsdp"), lax.axis_index("rep")
     count, width = patches.shape
-    rows = (count + RT - 1) // RT * RT
-    sh = width // parts
-
-    packed = pack_shards(*(m.astype(BF) for m in masters[:4]), parts).reshape(12 * sh, width)
-    piece = 12 * sh // copies
-    quarter = lax.dynamic_slice_in_dim(packed, copy * piece, piece, 0)
-    full = lax.all_gather(quarter, ("fsdp", "rep"), axis=0, tiled=True)
-    full = full.reshape(parts, 12, sh, width).swapaxes(0, 1).reshape(12, width, width)
-    vec = lax.all_gather(vector_weight.astype(BF), "fsdp", axis=1, tiled=True).astype(F32)
-    be = vec[6:].reshape(parts, 4, sh).swapaxes(0, 1).reshape(4, width)
-    vec = jnp.concatenate([vec[:6], be, jnp.zeros((6, width), F32)], axis=0)
-
-    pad = ((0, rows - count), (0, 0))
-    live = jnp.repeat(slot_clip >= 0, SLOT)[:, None]
-    x = jnp.pad(patches, pad)
-    dy = jnp.pad(jnp.where(live, out_grad, 0), pad)
-    t, a1 = run_qkv(x, vec, full[0:3])
-    o = attend(slot_clip, t)
-    out, dm, do, gwo, gwe, gwc, sums_two, sums_be = run_feed(x, o, dy, vec, full[3], full[4:8], full[8:12])
-    dt = attend_back(slot_clip, t, do)
-    pg, gwi, sums_one = run_first(x, a1, dt, dm, vec, full[0:3])
-
-    grads = jnp.concatenate([gwi, gwo[None], gwe, gwc], axis=0)
-    grads = grads.reshape(12, parts, sh, width).swapaxes(0, 1).reshape(parts * 12 * sh, width)
-    grads = lax.psum_scatter(grads, ("fsdp", "rep"), scatter_dimension=0, tiled=True)
-    grads = lax.all_gather(grads, "rep", axis=0, tiled=True).reshape(12, sh, width)
-    be_grad = sums_be[::8].reshape(4, parts, sh).swapaxes(0, 1).reshape(4, width)
-    vector = jnp.concatenate(
-        [sums_one[0:2], sums_two[2:3], sums_two[0:2], sums_two[3:4], be_grad], axis=0
-    )
-    vector = lax.dynamic_slice_in_dim(lax.psum(vector, ("fsdp", "rep")), mine * sh, sh, 1)
-    total_grads = tuple(g.astype(F32) for g in unpack_shards(grads, parts)) + (vector,)
+    direct = copies == 4 and parts % 4 == 0 and width // parts % 48 == 0
+    path = direct_path if direct else plain_path
+    out, pg, total_grads = path(patches, slot_clip, out_grad, masters[:4], vector_weight)
 
     tokens_all = count * parts * copies
-    outputs = [out[:count], pg[:count]]
+    outputs = [out, pg]
     for member in range(5):
         grad_sum = total_grads[member]
         rate = RATES[member] / tokens_all**0.5

time: 552 us -> 385 us (0.70)
  waiting for transfers between devices: 228 us -> 0 us
  Pallas kernels: 149 us -> 331 us
  blocking collectives: 72.7 us -> 0 us
  local copies, waits for them, and re-layouts: 54 us -> 29.1 us
  between operations: 14.4 us -> 1.31 us
  other arithmetic: 27.9 us -> 20.2 us
    pallas_call x4, Pallas kernels: 112 us -> 294 us  [the longest x3 273 us: comm_call(): pl.pallas_call(kernel, out_shape=[jax.ShapeDtypeStruct(s, d) for s, d in...]
    reduce_scatter x1 -> x0, waiting for transfers between devices: 161 us -> none  [on_device(): lax.psum_scatter(grads, ('fsdp', 'rep'), scatter_dimension=0, tiled=True)]
    all_gather x2 -> x0, waiting for transfers between devices: 66.9 us -> none  [the longest x1 66.9 us: on_device(): full = lax.all_gather(quarter, ('fsdp', 'rep'), axis=0, tiled=True)]
    psum x1 -> x0, blocking collectives: 40.1 us -> none  [on_device(): lax.psum(vector, ('fsdp', 'rep'))]
    all_gather x1 -> x0, blocking collectives: 32.6 us -> none  [on_device(): lax.all_gather(vector_weight.astype(BF), 'fsdp', axis=1, tiled=True)]
    slice x15 -> x11, local copies, waits for them, and re-layouts: 29 us -> 11.6 us  [the longest x2 5.47 us: direct_path(): return (out[:count], pg[:count], grads)]
    transpose x1 -> x0, other arithmetic: 7.15 us -> none  [on_device(): grads.reshape(12, parts, sh, width).swapaxes(0, 1)]
    transpose x4 -> x0, local copies, waits for them, and re-layouts: 6.51 us -> none  [the longest x1 5.59 us: on_device(): grads.reshape(12, parts, sh, width).swapaxes(0, 1)]
  transfers between devices with their start and end apart: 3 -> 0, of which waited for: 2 -> 0; matrix products, arithmetic and copies ran while one was open for 3% -> 0% of each run, Pallas kernels for 0% -> 0%
where the time goes in v2:
time: 385 us; the launch traced here: 381 us
  Pallas kernels  331 us (86%)
  local copies, waits for them, and re-layouts  29.1 us (8%)
  other arithmetic  20.2 us (5%)
    pallas_call x3, Pallas kernels, comm_call(): pl.pallas_call(kernel, out_shape=[jax.ShapeDtypeStruct(s, d) for s, d in...  273 us
    pallas_call x1, Pallas kernels, attend_back(): pl.pallas_call(bwd_kernel, out_shape=jax.ShapeDtypeStruct(t.shape, BF), i...  36.8 us
    pallas_call x1, Pallas kernels, attend(): pl.pallas_call(fwd_kernel, out_shape=[jax.ShapeDtypeStruct((t.shape[0], D...  21.2 us
    unnamed x66, local copies, waits for them, and re-layouts  10.6 us
    convert_element_type x5, other arithmetic, on_device(): weight_new.astype(BF)  8.41 us

profile of v2, /device:TPU:0, one launch (start us, length us, event | category | flops | bytes accessed | tf_op | source)
XLA Modules:
  0.0 381.3 jit_solution(15111636149068915325)
XLA Ops:
  3.7 1.3 convert_element_type.68
  5.3 1.4 copy-done.8
  9.8 1.0 pad_maximum_fusion.1
  10.8 58.9 %gather_project_in.1 = (bf16[1200,2304]{1,0:T(8,128)(2,1)}, bf16[1200,768]{1,0:T(8,128)(2,1)}, bf16[1200,768]{1,0:T(8,128)(2,1)}, bf16[6,4,2,96,768]{4,3,2,1,0:T(8,128)(2,1)}, f32[16,768]{1,0:T(8,128)}) custom-call(bf16[1176,768]{1,0:T(8,128)(2,1)} %x_ref.1, f32[16,768]{1,0:T(8,128)} %pad_maximum_fusion.2.vec_in, bf16[6,96,768]{2,1,0:T(8,128)(2,1)} %fusion.2.shard), custom_call_target="tpu_custom_call" | custom-call | tf_op jit(solution)/shard_map/gather_project_in/pallas_call | solution.py:800
  69.7 4.2 %slice.67.wi_ref = bf16[3,4,2,96,768]{4,3,2,1,0:T(8,128)(2,1)} slice(bf16[6,4,2,96,768]{4,3,2,1,0:T(8,128)(2,1)} %get-tuple-element.49), slice={[0:3], [0:4], [0:2], [0:96], [0:768]} | slice | bytes 7077888 | tf_op jit(solution)/shard_map/slice | solution.py:928
  73.9 1.2 copy-done.5
  75.1 1.9 fusion.9
  77.7 21.2 %attention_forward.1 = (bf16[1200,768]{1,0:T(8,128)(2,1)S(1)}, bf16[1200,768]{1,0:T(8,128)(2,1)S(1)}) custom-call(s32[24]{0:T(128)S(1)} %copy-done.4, bf16[1200,2304]{1,0:T(8,128)(2,1)} %get-tuple-element.45.t_ref, bf16[1176,768]{1,0:T(8,128)(2,1)S(1)} %copy-done.3), custom_call_target="tpu_custom_call" | custom-call | tf_op jit(solution)/shard_map/attention_forward/pallas_call | solution.py:130
  98.9 1.2 copy-done
  100.1 1.2 copy-done.1
  101.4 153.9 %feed_forward_reduce.1 = (bf16[1200,768]{1,0:T(8,128)(2,1)}, f32[1200,768]{1,0:T(8,128)}, bf16[1200,768]{1,0:T(8,128)(2,1)}, bf16[1200,768]{1,0:T(8,128)(2,1)}, ...) custom-call(bf16[1200,768]{1,0:T(8,128)(2,1)} %get-tuple-element.44.x_ref, ...), custom_call_target="tpu_custom_call" | custom-call | tf_op jit(solution)/shard_map/feed_forward_reduce/pallas_call | solution.py:800
  255.3 1.5 copy-done.2
  256.8 36.8 %attention_backward.1.dt_ref = bf16[1200,2304]{1,0:T(8,128)(2,1)} custom-call(s32[24]{0:T(128)S(1)} %copy-done.4, bf16[1200,2304]{1,0:T(8,128)(2,1)} %get-tuple-element.45.t_ref, bf16[1200,768]{1,0:T(8,128)(2,1)S(1)} %copy-done.2), custom_call_target="tpu_custom_call" | custom-call | tf_op jit(solution)/shard_map/attention_backward/pallas_call | solution.py:136
  293.6 59.8 %project_in_back_reduce.1 = (f32[1200,768]{1,0:T(8,128)}, bf16[4,96,768]{2,1,0:T(8,128)(2,1)}, f32[16,768]{1,0:T(8,128)}) custom-call(bf16[1200,768]{1,0:T(8,128)(2,1)} %get-tuple-element.44.x_ref, bf16[1200,768]{1,0:T(8,128)(2,1)} %get-tuple-element.51.a1_ref, bf16[1200,768]{1,0:T(8,128)(2,1)} %copy-done, bf16[1200,768]{1,0:T(8,128)(2,1)} %get-tuple-element.52.dz_ref, ...), custom_call_target="tpu_custom_call" | custom-call | tf_op jit(solution)/shard_map/project_in_back_reduce/pallas_call | solution.py:800
  353.5 1.3 slice.66
  354.8 4.1 %slice.68 = f32[1176,768]{1,0:T(8,128)} slice(f32[1200,768]{1,0:T(8,128)} %get-tuple-element.57), slice={[0:1176], [0:768]} | slice | bytes 7225344 | tf_op jit(solution)/shard_map/slice | solution.py:939
  365.1 1.0 copy.52
  366.2 1.6 reshape.166
  367.8 3.4 fusion.8
  371.2 1.0 add_multiply_fusion.2
  373.5 1.6 fusion.6
  375.1 1.1 add_multiply_fusion.1
  377.7 1.9 fusion.5
  379.6 1.3 add_multiply_fusion
  (106 shorter events, 15.9 us)
Async XLA Ops:
  3.7 1.5 copy-start.10
  5.3 1.5 copy-start.15
  69.7 5.4 %copy-start.5 = (bf16[6,4,2,96,768]{4,3,2,1,0:T(8,128)(2,1)S(1)}, bf16[6,4,2,96,768]{4,3,2,1,0:T(8,128)(2,1)}, u32[]{:S(2)}) copy-start(bf16[6,4,2,96,768]{4,3,2,1,0:T(8,128)(2,1)} %get-tuple-element.49) | copy-start | bytes 21233668
  75.1 2.6 copy-start.3
  75.1 2.6 copy-start.4
  255.3 1.5 copy-start.2
  293.6 59.9 %copy-start.16 = (bf16[1200,768]{1,0:T(8,128)(2,1)S(1)}, bf16[1200,768]{1,0:T(8,128)(2,1)}, u32[]{:S(2)}) copy-start(bf16[1200,768]{1,0:T(8,128)(2,1)} %get-tuple-element.50) | copy-start | bytes 5529604
  354.8 4.2 %copy-start.30 = (f32[16,768]{1,0:T(8,128)S(1)}, f32[16,768]{1,0:T(8,128)}, u32[]{:S(2)}) copy-start(f32[16,768]{1,0:T(8,128)} %get-tuple-element.60) | copy-start | bytes 147460
  354.8 4.4 %copy-start.29 = (f32[10,96]{1,0:T(8,128)S(1)}, f32[10,96]{1,0:T(8,128)}, u32[]{:S(2)}) copy-start(f32[10,96]{1,0:T(8,128)} %param.33) | copy-start | bytes 11524
  354.8 4.4 %copy-start.31 = (f32[10,96]{1,0:T(8,128)S(1)}, f32[10,96]{1,0:T(8,128)}, u32[]{:S(2)}) copy-start(f32[10,96]{1,0:T(8,128)} %param.34) | copy-start | bytes 11524
  354.8 5.0 %copy-start.32 = (f32[10,96]{1,0:T(8,128)S(1)}, f32[10,96]{1,0:T(8,128)}, u32[]{:S(2)}) copy-start(f32[10,96]{1,0:T(8,128)} %param.35) | copy-start | bytes 11524
  354.8 5.6 %copy-start.25 = (bf16[4,96,768]{2,1,0:T(8,128)(2,1)S(1)}, bf16[4,96,768]{2,1,0:T(8,128)(2,1)}, u32[]{:S(2)}) copy-start(bf16[4,96,768]{2,1,0:T(8,128)(2,1)} %get-tuple-element.58) | copy-start | bytes 1769476
  359.8 1.7 copy-start.28
  361.7 1.8 copy-start.23
  362.6 1.8 copy-start.21
  367.8 4.5 %copy-start.12 = (f32[96,3072]{1,0:T(8,128)}, f32[96,3072]{1,0:T(8,128)S(1)}, u32[]{:S(2)}) copy-start(f32[96,3072]{1,0:T(8,128)S(1)} %reshape.166) | copy-start | bytes 3538948
  367.8 3.4 copy-start.24
  371.2 1.9 copy-start.9
  371.2 2.3 copy-start.17
  373.5 1.6 copy-start.18
  375.1 2.1 copy-start.11
  375.1 2.3 copy-start.14
  375.1 2.6 copy-start.19
  377.7 1.9 copy-start.20
  (10 other events, 12.8 us)

commit v3 on v2

--- a/solution.py
+++ b/solution.py
@@ -625,7 +625,7 @@
         sent(self.far())
 
 
-FIRST_BLOCKS = 6
+FIRST_BLOCKS = 8
 TILES = 3
 
 
@@ -634,7 +634,9 @@
     return block.reshape(block.shape[0] * block.shape[1] * block.shape[2], block.shape[3])
 
 
-def gather_kernel(parts, x_ref, vec_in, shard, t_ref, a1_ref, xp_ref, full, vec, *scratch):
+def gather_kernel(
+    parts, x_ref, vec_in, shard, t_out, a1_ref, xp_ref, wi_out, wo_out, ff_out, vec, t_ref, full, local, *scratch
+):
     count, width = x_ref.shape
     rows = xp_ref.shape[0]
     place = Place(parts, shard.shape[1], width)
@@ -653,37 +655,48 @@
     weights.step(2, FIRST_BLOCKS, 1)
     qkv_norm(xp_ref, vec, a1_ref)
     weights.step(3, FIRST_BLOCKS, 1)
+    leaving = []
     for s in range(4, FIRST_BLOCKS + 4):
+        b = s - 4
         weights.step(s, FIRST_BLOCKS, 1)
-        if s - 4 < 3:
-            qkv_block(a1_ref, full, t_ref, s - 4)
+        out = wi_out.at[b] if b < 3 else wo_out.at[0] if b == 3 else ff_out.at[b - 4]
+        leaving.append(pltpu.make_async_copy(full.at[b], out, local.at[b]))
+        leaving[-1].start()
+        if b < 3:
+            qkv_block(a1_ref, full, t_ref, b)
+            part = pl.ds(b * width, width)
+            leaving.append(pltpu.make_async_copy(t_ref.at[:, part], t_out.at[:, part], local.at[FIRST_BLOCKS + b]))
+            leaving[-1].start()
+    for copy in leaving:
+        copy.wait()
     weights.finish(FIRST_BLOCKS)
     vectors.finish()
 
 
 def feed_comm_kernel(
-    parts, x_ref, o_ref, dy_ref, vec, wo_ref, we0_ref, wc0_ref, shard,
+    parts, x_ref, o_ref, dy_ref, vec, wo_ref, early, shard,
     out_ref, dm_ref, do_ref, dz_ref, grad_out, sums, be_ref,
     a2_ref, y_ref, da2_ref, full, grad, local, *scratch,
 ):
     rows, width = x_ref.shape
     sh = shard.shape[1]
     place = Place(parts, sh, width)
-    later = shard.shape[0]
-    weights = Gather(place, shard, full.at[pl.ds(2, later)], scratch[0:2])
+    later, have = shard.shape[0], early.shape[0]
+    weights = Gather(place, shard, full.at[pl.ds(have, later)], scratch[0:2])
     grads = Reduce(place, grad, grad_out, scratch[2:8], scratch[8:10])
+    du_ref, h_ref = do_ref, dz_ref
+    ready = pltpu.make_async_copy(early, full.at[pl.ds(0, have)], local)
+    ready.start()
     place.greet()
-    du_ref, h_ref = do_ref, dz_ref
-    ready = [
-        pltpu.make_async_copy(ref.at[0], full.at[b], local.at[b]) for b, ref in enumerate((we0_ref, wc0_ref))
-    ]
-    start(ready)
 
     def win(i):
         return pl.ds(i * RT, RT)
 
+    def slot(number):
+        weights.step(number, later, 3)
+
     wo = flat(wo_ref, 0)
-    weights.step(0, later, 1)
+    slot(0)
     for i in range(TILES):
         middle = x_ref[win(i), :].astype(F32) + (dot_nn(o_ref[win(i), :], wo) + vec[2:3, :])
         dm_ref[win(i), :] = middle
@@ -691,21 +704,25 @@
         a2_ref[win(i), :] = (unit * vec[3:4, :] + vec[4:5, :]).astype(BF)
         y_ref[win(i), :] = jnp.zeros((RT, width), F32)
         da2_ref[win(i), :] = jnp.zeros((RT, width), F32)
-        weights.step(i + 1, later, 1)
-    for copy in ready:
-        copy.wait()
-
-    def passing(j, i):
-        for parity in range(2):
-            for back in range(3):
-                stage = i - 3 - parity + 5 * back
-                if 0 <= stage <= 6:
-                    if back == 0:
-                        grads.stage(2 * j + parity, stage)
-                    else:
-                        @pl.when(j >= back)
-                        def _():
-                            grads.stage(2 * (j - back) + parity, stage)
+        slot(i + 1)
+    ready.wait()
+
+    def due(position, back, parity):
+        steps = position - 3 - parity + 5 * back
+        return steps // 2 if steps % 2 == 0 and 0 <= steps <= 12 else None
+
+    def passing(j, position):
+        for back in range(3, -1, -1):
+            for parity in range(2):
+                stage = due(position, back, parity)
+                if stage is None:
+                    continue
+                if back == 0:
+                    grads.stage(2 * j + parity, stage)
+                else:
+                    @pl.when(j >= back)
+                    def _():
+                        grads.stage(2 * (j - back) + parity, stage)
 
     @pl.loop(0, 4)
     def _(j):
@@ -720,19 +737,19 @@
             be_sum += column_sum(du.astype(F32))
             y_ref[win(i), :] += dot_nn(hidden, flat(full, 2 * j + 1))
             da2_ref[win(i), :] += dot_nt(du, flat(full, 2 * j))
-            weights.step(4 + 5 * j + i, later, 1)
+            slot(4 + 5 * j + i)
             passing(j, i)
         be_ref[pl.ds(j, 1), :] = be_sum
         grad[2 * j] = dot_tn(h_ref[...], dy_ref[...]).astype(BF).reshape(grad.shape[1:])
-        weights.step(4 + 5 * j + 3, later, 1)
+        slot(4 + 5 * j + 3)
         passing(j, 3)
         grad[2 * j + 1] = dot_tn(a2_ref[...], du_ref[...]).astype(BF).reshape(grad.shape[1:])
-        weights.step(4 + 5 * j + 4, later, 1)
+        slot(4 + 5 * j + 4)
         passing(j, 4)
 
     sums[...] = jnp.zeros_like(sums)
-    for slot in range(5, 12):
-        i = slot - 5
+    for position in range(5, 17):
+        i = position - 5
         if i < TILES:
             middle = dm_ref[win(i), :]
             out_ref[win(i), :] = (middle + (y_ref[win(i), :] + vec[5:6, :])).astype(BF)
@@ -748,10 +765,10 @@
             sums[1:2, :] += column_sum(da2)
             sums[2:3, :] += column_sum(dz.astype(F32))
             sums[3:4, :] += column_sum(dy)
-        for j in range(2, 4):
+        for j in range(1, 4):
             for parity in range(2):
-                stage = slot - 3 - parity + 5 * (3 - j)
-                if 0 <= stage <= 6:
+                stage = due(position + 5 * (3 - j), 0, parity)
+                if stage is not None:
                     grads.stage(2 * j + parity, stage)
     weights.finish(later)
     grads.finish(8)
@@ -796,18 +813,83 @@
     vectors.finish()
 
 
-def comm_call(kernel, name, which, ins, outs, scratch, far=()):
+def comm_call(kernel, name, which, ins, outs, scratch, far=(), far_out=()):
     return pl.pallas_call(
         kernel,
         out_shape=[jax.ShapeDtypeStruct(s, d) for s, d in outs],
         in_specs=[pl.BlockSpec(memory_space=pl.ANY) if i in far else VM for i in range(len(ins))],
-        out_specs=[VM] * len(outs),
+        out_specs=[pl.BlockSpec(memory_space=pl.ANY) if i in far_out else VM for i in range(len(outs))],
         scratch_shapes=scratch,
         compiler_params=pltpu.CompilerParams(
             vmem_limit_bytes=62 * 2**20, collective_id=which, has_side_effects=True
         ),
         name=name,
     )(*ins)
+
+
+STEPS = 6
+
+
+def update_kernel(rates, g_one, g_two, *refs):
+    state, outs, flat_we = refs[:12], refs[12:32], refs[32]
+    i = pl.program_id(0)
+    sh, width = g_two.shape[1:]
+    parts = width // sh
+
+    @pl.when(i == 0)
+    def _():
+        for j in range(4):
+            for p in range(parts):
+                flat_we[:, pl.ds((4 * p + j) * sh, sh)] = g_two[2 * j + 1, :, pl.ds(p * sh, sh)].astype(F32)
+
+    half, sixth = width // 2, width // STEPS
+    odd = pl.ds(pl.multiple_of(i % 2 * half, 128), half)
+    third = sh // 3
+    pieces = [g_two[2 * (k // 3), pl.ds(pl.multiple_of(k % 3 * third, 16), third), :] for k in (2 * i, 2 * i + 1)]
+    sums = (
+        g_one[1 + i // 2, :, odd].astype(F32),
+        g_one[0, :, pl.ds(pl.multiple_of(i * sixth, 128), sixth)].astype(F32),
+        flat_we[:, pl.ds(pl.multiple_of(i * 4 * sixth, 128), 4 * sixth)],
+        jnp.concatenate(pieces, axis=0).astype(F32),
+    )
+    for member in range(4):
+        weight, moment, average = (ref[...] for ref in state[3 * member : 3 * member + 3])
+        grad, moment_out, weight_out, average_out, low_out = outs[5 * member : 5 * member + 5]
+        total = sums[member]
+        grad[...] = total
+        moment_new = MOMENTUM * moment + total
+        weight_new = weight - rates[member] * (total + MOMENTUM * moment_new)
+        moment_out[...] = moment_new
+        weight_out[...] = weight_new
+        average_out[...] = AVERAGE * average + (1.0 - AVERAGE) * weight_new
+        low_out[...] = weight_new.astype(BF)
+
+
+def update(rates, g_one, g_two, masters, moments, averages):
+    sh, width = g_two.shape[1:]
+    across = [
+        pl.BlockSpec((sh, width // 2), lambda i: (0, i)),
+        pl.BlockSpec((sh, width // STEPS), lambda i: (0, i)),
+        pl.BlockSpec((sh, 4 * width // STEPS), lambda i: (0, i)),
+        pl.BlockSpec((4 * sh // STEPS, width), lambda i: (i, 0)),
+    ]
+    ins, specs, outs, out_specs = [], [], [], []
+    for member in range(4):
+        ins += [masters[member], moments[member], averages[member]]
+        specs += [across[member]] * 3
+        shape = masters[member].shape
+        outs += [jax.ShapeDtypeStruct(shape, F32)] * 4 + [jax.ShapeDtypeStruct(shape, BF)]
+        out_specs += [across[member]] * 5
+    return pl.pallas_call(
+        functools.partial(update_kernel, rates),
+        grid=(STEPS,),
+        out_shape=outs,
+        in_specs=[pl.BlockSpec(g.shape, lambda i: (0, 0, 0)) for g in (g_one, g_two)] + specs,
+        out_specs=out_specs,
+        scratch_shapes=[pltpu.VMEM((sh, 4 * width), F32)],
+        compiler_params=pltpu.CompilerParams(vmem_limit_bytes=48 * 2**20),
+        name="momentum_step",
+    )(g_one, g_two, *ins)
 
 
 def run_qkv(x, vec, wi):
@@ -851,7 +933,14 @@
     return wi, blocks[3], we, blocks[8:12].reshape(4 * rows, width)
 
 
-def plain_path(patches, slot_clip, out_grad, masters, vector_weight):
+def step(grad_sum, rate, weight, moment, average):
+    moment_new = MOMENTUM * moment + grad_sum
+    weight_new = weight - rate * (grad_sum + MOMENTUM * moment_new)
+    average_new = AVERAGE * average + (1.0 - AVERAGE) * weight_new
+    return [grad_sum, moment_new, weight_new, average_new, weight_new.astype(BF)]
+
+
+def plain_path(patches, slot_clip, out_grad, masters, moments, averages, rates, vector_weight):
     parts, copies = lax.axis_size("fsdp"), lax.axis_size("rep")
     mine, copy = lax.axis_index("fsdp"), lax.axis_index("rep")
     count, width = patches.shape
@@ -883,10 +972,13 @@
         [sums_one[0:2], sums_two[2:3], sums_two[0:2], sums_two[3:4], be_grad], axis=0
     )
     vector = lax.dynamic_slice_in_dim(lax.psum(vector, ("fsdp", "rep")), mine * sh, sh, 1)
-    return out[:count], pg[:count], tuple(g.astype(F32) for g in unpack_shards(grads, parts)) + (vector,)
-
-
-def direct_path(patches, slot_clip, out_grad, masters, vector_weight):
+    outputs = []
+    for member, grad in enumerate(unpack_shards(grads, parts)):
+        outputs += step(grad.astype(F32), rates[member], masters[member], moments[member], averages[member])
+    return out[:count], pg[:count], vector, outputs
+
+
+def direct_path(patches, slot_clip, out_grad, masters, moments, averages, rates, vector_weight):
     parts = lax.axis_size("fsdp")
     mine = lax.axis_index("fsdp")
     count, width = patches.shape
@@ -896,9 +988,8 @@
     wide, low = ((rows, width), F32), ((rows, width), BF)
 
     packed = pack_shards(*(m.astype(BF) for m in masters), parts)
-    first = jnp.concatenate([packed[0:5], packed[8:9]], axis=0)
-    later = packed[5:8], packed[9:12]
-    later = jnp.stack(later, axis=1).reshape(6, sh, width)
+    first = jnp.concatenate([packed[0:5], packed[8:9], packed[5:6], packed[9:10]], axis=0)
+    later = jnp.stack((packed[6:8], packed[10:12]), axis=1).reshape(4, sh, width)
     vector_low = vector_weight.astype(BF).astype(F32)
     place = jnp.arange(parts)[None, :, None]
     row = jnp.arange(4)[:, None, None]
@@ -908,35 +999,37 @@
     be = jnp.where((row == mine % 4) & (place % apart == mine // 4), be, 0.0)
     placed = jnp.concatenate([top, be, jnp.zeros((6, parts, sh), F32)], axis=0).reshape(16, width)
 
-    t, a1, x, full, vec = comm_call(
+    t, a1, x, wi, wo, early, vec = comm_call(
         functools.partial(gather_kernel, parts), "gather_project_in", 0, (patches, placed, first),
-        [((rows, 3 * width), BF), low, low, ((FIRST_BLOCKS,) + block, BF), ((16, width), F32)],
-        gather_sems(FIRST_BLOCKS, parts) + Vector.scratch(parts, (16, width), F32),
+        [((rows, 3 * width), BF), low, low, ((3,) + block, BF), ((1,) + block, BF),
+         ((FIRST_BLOCKS - 4,) + block, BF), ((16, width), F32)],
+        [pltpu.VMEM((rows, 3 * width), BF), pltpu.VMEM((FIRST_BLOCKS,) + block, BF),
+         pltpu.SemaphoreType.DMA((FIRST_BLOCKS + 3,))]
+        + gather_sems(FIRST_BLOCKS, parts) + Vector.scratch(parts, (16, width), F32),
+        far_out=(0, 3, 4, 5),
     )
     o, dy = attend(slot_clip, t, out_grad)
     out, dm, do, dz, grads_two, sums_two, sums_be = comm_call(
         functools.partial(feed_comm_kernel, parts), "feed_forward_reduce", 1,
-        (x, o, dy, vec, full[3:4], full[4:5], full[5:6], later),
+        (x, o, dy, vec, wo, early, later),
         [low, wide, low, low, ((8, sh, width), BF), ((8, width), F32), ((8, width), F32)],
         [pltpu.VMEM(*low), pltpu.VMEM(*wide), pltpu.VMEM(*wide),
-         pltpu.VMEM((8,) + block, BF), pltpu.VMEM((8,) + block, BF), pltpu.SemaphoreType.DMA((2,))]
-        + gather_sems(6, parts) + Reduce.scratch(8, parts, sh, width), far=(5, 6),
+         pltpu.VMEM((8,) + block, BF), pltpu.VMEM((8,) + block, BF), pltpu.SemaphoreType.DMA]
+        + gather_sems(4, parts) + Reduce.scratch(8, parts, sh, width), far=(5,),
     )
     dt = attend_back(slot_clip, t, do)
     pg, grads_one, vector = comm_call(
         functools.partial(first_comm_kernel, parts), "project_in_back_reduce", 2,
-        (x, a1, o, dz, dt, dm, vec, full[0:3], sums_two, sums_be),
+        (x, a1, o, dz, dt, dm, vec, wi, sums_two, sums_be),
         [wide, ((4, sh, width), BF), ((16, width), F32)],
         [pltpu.VMEM((4,) + block, BF)] + Reduce.scratch(4, parts, sh, width)
         + Vector.scratch(parts, (16, width), F32),
     )
-    blocks = jnp.concatenate([grads_one[1:4], grads_one[0:1], grads_two[1::2], grads_two[0::2]], axis=0)
     top = lax.dynamic_slice_in_dim(vector[:6], mine * sh, sh, 1)
     be = lax.dynamic_slice_in_dim(vector, 6 + mine % 4, 1, 0).reshape(4, apart, sh)
     be = lax.dynamic_index_in_dim(be, mine // 4, 1, keepdims=False)
     vector = jnp.concatenate([top, be], axis=0)
-    grads = tuple(g.astype(F32) for g in unpack_shards(blocks, parts)) + (vector,)
-    return out[:count], pg[:count], grads
+    return out[:count], pg[:count], vector, update(rates, grads_one, grads_two, masters, moments, averages)
 
 
 def on_device(
@@ -954,18 +1047,12 @@
     count, width = patches.shape
     direct = copies == 4 and parts % 4 == 0 and width // parts % 48 == 0
     path = direct_path if direct else plain_path
-    out, pg, total_grads = path(patches, slot_clip, out_grad, masters[:4], vector_weight)
-
     tokens_all = count * parts * copies
-    outputs = [out, pg]
-    for member in range(5):
-        grad_sum = total_grads[member]
-        rate = RATES[member] / tokens_all**0.5
-        moment_new = MOMENTUM * moments[member] + grad_sum
-        weight_new = masters[member] - rate * (grad_sum + MOMENTUM * moment_new)
-        average_new = AVERAGE * averages[member] + (1.0 - AVERAGE) * weight_new
-        outputs.extend([grad_sum, moment_new, weight_new, average_new, weight_new.astype(BF)])
-    return tuple(outputs)
+    rates = [rate / tokens_all**0.5 for rate in RATES]
+    out, pg, vector, outputs = path(
+        patches, slot_clip, out_grad, masters[:4], moments[:4], averages[:4], rates, vector_weight
+    )
+    return (out, pg, *outputs, *step(vector, rates[4], masters[4], moments[4], averages[4]))
 
 
 def solution(mesh):

time: 385 us -> 348 us (0.904)
  Pallas kernels: 331 us -> 316 us
  other arithmetic: 20.2 us -> 8.34 us
  local copies, waits for them, and re-layouts: 29.1 us -> 18.2 us
    pallas_call x3, Pallas kernels: 273 us -> 249 us  [comm_call(): pl.pallas_call(kernel, out_shape=[jax.ShapeDtypeStruct(s, d) for s, d in...]
    pallas_call x0 -> x1, Pallas kernels: none -> 9.94 us  [update(): pl.pallas_call(functools.partial(update_kernel, rates), grid=(STEPS,), ou...]
    convert_element_type x5 -> x1, other arithmetic: 8.41 us -> 1.31 us  [step(): weight_new.astype(BF)]
    slice x8, local copies, waits for them, and re-layouts: 11.6 us -> 5.8 us  [the longest x1 4.22 us: direct_path(): pg[:count]]
    convert_element_type x4 -> x0, local copies, waits for them, and re-layouts: 4.31 us -> none  [direct_path(): g.astype(F32)]
    unnamed x66 -> x40, local copies, waits for them, and re-layouts: 10.6 us -> 8.55 us
where the time goes in v3:
time: 348 us; the launch traced here: 344 us
  Pallas kernels  316 us (91%)
  local copies, waits for them, and re-layouts  18.2 us (5%)
  other arithmetic  8.34 us (2%)
    pallas_call x3, Pallas kernels, comm_call(): pl.pallas_call(kernel, out_shape=[jax.ShapeDtypeStruct(s, d) for s, d in...  249 us
    pallas_call x1, Pallas kernels, attend_back(): pl.pallas_call(bwd_kernel, out_shape=jax.ShapeDtypeStruct(t.shape, BF), i...  36.8 us
    pallas_call x1, Pallas kernels, attend(): pl.pallas_call(fwd_kernel, out_shape=[jax.ShapeDtypeStruct((t.shape[0], D...  21.2 us
    pallas_call x1, Pallas kernels, update(): pl.pallas_call(functools.partial(update_kernel, rates), grid=(STEPS,), ou...  9.94 us
    unnamed x40, local copies, waits for them, and re-layouts  8.55 us

profile of v3, /device:TPU:0, one launch (start us, length us, event | category | flops | bytes accessed | tf_op | source)
XLA Modules:
  0.0 344.3 jit_solution(3966425257534268789)
XLA Ops:
  1.2 0.7 convert_convert_fusion
  2.7 1.0 convert_bitcast_fusion
  3.7 1.2 convert_element_type.23
  5.1 1.3 copy-done.13
  6.5 0.8 reshape.148
  8.2 1.1 fusion.4.shard
  9.7 0.9 pad_maximum_fusion.1
  10.5 66.2 %gather_project_in.1 = (bf16[1200,2304]{1,0:T(8,128)(2,1)}, bf16[1200,768]{1,0:T(8,128)(2,1)}, bf16[1200,768]{1,0:T(8,128)(2,1)}, bf16[3,4,2,96,768]{4,3,2,1,0:T...) custom-call(bf16[1176,768]{1,0:T(8,128)(2,1)} %x_ref.1, ...), custom_call_target="tpu_custom_call" | custom-call | tf_op jit(solution)/shard_map/gather_project_in/pallas_call | solution.py:817
  76.8 21.2 %attention_forward.1 = (bf16[1200,768]{1,0:T(8,128)(2,1)S(1)}, bf16[1200,768]{1,0:T(8,128)(2,1)S(1)}) custom-call(s32[24]{0:T(128)S(1)} %copy-done.12, bf16[1200,2304]{1,0:T(8,128)(2,1)} %get-tuple-element.67.t_ref, bf16[1176,768]{1,0:T(8,128)(2,1)S(1)} %copy-done.4), custom_call_target="tpu_custom_call" | custom-call | tf_op jit(solution)/shard_map/attention_forward/pallas_call | solution.py:130
  98.0 1.2 copy-done
  99.3 1.3 copy-done.2
  100.5 123.9 %feed_forward_reduce.1 = (bf16[1200,768]{1,0:T(8,128)(2,1)}, f32[1200,768]{1,0:T(8,128)}, bf16[1200,768]{1,0:T(8,128)(2,1)}, bf16[1200,768]{1,0:T(8,128)(2,1)}, ...) custom-call(bf16[1200,768]{1,0:T(8,128)(2,1)} %get-tuple-element.66.x_ref, ...), custom_call_target="tpu_custom_call" | custom-call | tf_op jit(solution)/shard_map/feed_forward_reduce/pallas_call | solution.py:817
  224.4 1.5 copy-done.3
  225.9 36.8 %attention_backward.1.dt_ref = bf16[1200,2304]{1,0:T(8,128)(2,1)} custom-call(s32[24]{0:T(128)S(1)} %copy-done.12, bf16[1200,2304]{1,0:T(8,128)(2,1)} %get-tuple-element.67.t_ref, bf16[1200,768]{1,0:T(8,128)(2,1)S(1)} %copy-done.3), custom_call_target="tpu_custom_call" | custom-call | tf_op jit(solution)/shard_map/attention_backward/pallas_call | solution.py:136
  262.7 58.4 %project_in_back_reduce.1 = (f32[1200,768]{1,0:T(8,128)}, bf16[4,96,768]{2,1,0:T(8,128)(2,1)}, f32[16,768]{1,0:T(8,128)}) custom-call(bf16[1200,768]{1,0:T(8,128)(2,1)} %get-tuple-element.66.x_ref, bf16[1200,768]{1,0:T(8,128)(2,1)} %get-tuple-element.74.a1_ref, bf16[1200,768]{1,0:T(8,128)(2,1)} %copy-done, bf16[1200,768]{1,0:T(8,128)(2,1)} %get-tuple-element.75.dz_ref, ...), custom_call_target="tpu_custom_call" | custom-call | tf_op jit(solution)/shard_map/project_in_back_reduce/pallas_call | solution.py:817
  321.1 1.3 slice.55
  322.5 4.2 %slice.56 = f32[1176,768]{1,0:T(8,128)} slice(f32[1200,768]{1,0:T(8,128)} %get-tuple-element.81), slice={[0:1176], [0:768]} | slice | bytes 7225344 | tf_op jit(solution)/shard_map/slice | solution.py:1032
  327.5 0.7 constant_dynamic-slice_fusion
  328.2 1.3 fusion.6
  329.5 1.3 add_multiply_fusion
  330.9 1.2 copy-done.8
  332.0 1.1 copy-done.9
  333.1 1.0 copy-done.11
  334.1 9.9 %momentum_step.1 = (f32[96,2304]{1,0:T(8,128)}, f32[96,2304]{1,0:T(8,128)}, f32[96,2304]{1,0:T(8,128)}, f32[96,2304]{1,0:T(8,128)}, bf16[96,2304]{1,0:T(8,128)(2...) custom-call(bf16[4,96,768]{2,1,0:T(8,128)(2,1)S(1)} %copy-done.9, ...), custom_call_target="tpu_custom_call" | custom-call | tf_op jit(solution)/shard_map/momentum_step/pallas_call | solution.py:883
  (67 shorter events, 3.6 us)
Async XLA Ops:
  0.7 4.3 %copy-start.14 = (f32[384,768]{1,0:T(8,128)S(1)}, f32[384,768]{1,0:T(8,128)}, u32[]{:S(2)}) copy-start(f32[384,768]{1,0:T(8,128)} %refs_9_.1) | copy-start | bytes 3538948
  4.9 1.5 copy-start.13
  5.0 2.2 copy-start.15
  8.2 1.4 slice-start
  10.5 66.2 %copy-start.4 = (bf16[1176,768]{1,0:T(8,128)(2,1)S(1)}, bf16[1176,768]{1,0:T(8,128)(2,1)}, u32[]{:S(2)}) copy-start(bf16[1176,768]{1,0:T(8,128)(2,1)} %g_ref.1) | copy-start | bytes 5419012
  10.5 66.3 %copy-start.12 = (s32[24]{0:T(128)S(1)}, s32[24]{0:T(128)}, u32[]{:S(2)}) copy-start(s32[24]{0:T(128)} %clips.3) | copy-start | bytes 292
  98.0 1.2 copy-start
  99.3 1.3 copy-start.2
  224.4 1.5 copy-start.3
  262.7 58.4 %copy-start.16 = (bf16[1200,768]{1,0:T(8,128)(2,1)S(1)}, bf16[1200,768]{1,0:T(8,128)(2,1)}, u32[]{:S(2)}) copy-start(bf16[1200,768]{1,0:T(8,128)(2,1)} %get-tuple-element.73) | copy-start | bytes 5529604
  322.5 4.3 %copy-start.19 = (f32[16,768]{1,0:T(8,128)S(1)}, f32[16,768]{1,0:T(8,128)}, u32[]{:S(2)}) copy-start(f32[16,768]{1,0:T(8,128)} %get-tuple-element.104) | copy-start | bytes 147460
  322.5 5.8 %copy-start.18 = (f32[10,96]{1,0:T(8,128)S(1)}, f32[10,96]{1,0:T(8,128)}, u32[]{:S(2)}) copy-start(f32[10,96]{1,0:T(8,128)} %param.33) | copy-start | bytes 11524
  322.5 8.4 %copy-start.1 = (f32[96,2304]{1,0:T(8,128)S(1)}, f32[96,2304]{1,0:T(8,128)}, u32[]{:S(2)}) copy-start(f32[96,2304]{1,0:T(8,128)} %refs_0_.1) | copy-start | bytes 2654212
  322.5 8.4 %copy-start.5 = (bf16[8,96,768]{2,1,0:T(8,128)(2,1)S(1)}, bf16[8,96,768]{2,1,0:T(8,128)(2,1)}, u32[]{:S(2)}) copy-start(bf16[8,96,768]{2,1,0:T(8,128)(2,1)} %get-tuple-element.83.g_two) | copy-start | bytes 3538948
  322.5 8.4 %copy-start.6 = (f32[96,768]{1,0:T(8,128)S(1)}, f32[96,768]{1,0:T(8,128)}, u32[]{:S(2)}) copy-start(f32[96,768]{1,0:T(8,128)} %refs_3_.1) | copy-start | bytes 884740
  322.5 8.4 %copy-start.7 = (f32[96,2304]{1,0:T(8,128)S(1)}, f32[96,2304]{1,0:T(8,128)}, u32[]{:S(2)}) copy-start(f32[96,2304]{1,0:T(8,128)} %refs_1_.1) | copy-start | bytes 2654212
  322.5 8.4 %copy-start.10 = (f32[96,768]{1,0:T(8,128)S(1)}, f32[96,768]{1,0:T(8,128)}, u32[]{:S(2)}) copy-start(f32[96,768]{1,0:T(8,128)} %refs_4_.1) | copy-start | bytes 884740
  329.5 14.5 %copy-start.17 = (f32[10,96]{1,0:T(8,128)}, f32[10,96]{1,0:T(8,128)S(1)}, u32[]{:S(2)}) copy-start(f32[10,96]{1,0:T(8,128)S(1)} %get-tuple-element.106) | copy-start | bytes 11524
  330.9 1.2 copy-start.8
  332.0 1.1 copy-start.9
  333.1 1.0 copy-start.11

commit v4 on v3

--- a/solution.py
+++ b/solution.py
@@ -438,14 +438,16 @@
         for stage in range(5):
             @pl.when((s >= stage * lag) & (s < count + stage * lag))
             def _():
-                b = s - stage * lag
-                if stage == 0:
-                    start(self.far(b))
-                    self.put_own(b)
-                else:
-                    landed(self.far(b) if stage == 1 else self.pair(b, stage - 2))
-                    if stage < 4:
-                        start(self.pair(b, stage - 1))
+                self.stage(s - stage * lag, stage)
+
+    def stage(self, b, stage):
+        if stage == 0:
+            start(self.far(b))
+            self.put_own(b)
+        else:
+            landed(self.far(b) if stage == 1 else self.pair(b, stage - 2))
+            if stage < 4:
+                start(self.pair(b, stage - 1))
 
     def finish(self, count):
         @pl.loop(0, count)
@@ -674,8 +676,8 @@
 
 
 def feed_comm_kernel(
-    parts, x_ref, o_ref, dy_ref, vec, wo_ref, early, shard,
-    out_ref, dm_ref, do_ref, dz_ref, grad_out, sums, be_ref,
+    parts, x_ref, o_ref, dy_ref, vec, wo_ref, early, last, shard,
+    out_ref, dm_ref, do_ref, dz_ref, grad_out, grad_rest, sums, be_ref,
     a2_ref, y_ref, da2_ref, full, grad, local, *scratch,
 ):
     rows, width = x_ref.shape
@@ -683,17 +685,28 @@
     place = Place(parts, sh, width)
     later, have = shard.shape[0], early.shape[0]
     weights = Gather(place, shard, full.at[pl.ds(have, later)], scratch[0:2])
-    grads = Reduce(place, grad, grad_out, scratch[2:8], scratch[8:10])
+    grads = Reduce(place, grad.at[pl.ds(0, have)], grad_out, scratch[2:8], scratch[8:10])
     du_ref, h_ref = do_ref, dz_ref
-    ready = pltpu.make_async_copy(early, full.at[pl.ds(0, have)], local)
-    ready.start()
+    ready = [pltpu.make_async_copy(early, full.at[pl.ds(0, have)], local.at[0])] + [
+        pltpu.make_async_copy(last.at[:, :, b], full.at[have + later + b], local.at[1 + b]) for b in range(2)
+    ]
+    start(ready)
     place.greet()
 
     def win(i):
         return pl.ds(i * RT, RT)
 
     def slot(number):
-        weights.step(number, later, 3)
+        for b in range(2):
+            for stage, at in enumerate((0, 4, 7, 10, 12)):
+                due = at + b
+                if isinstance(number, int):
+                    if due == number:
+                        weights.stage(b, stage)
+                elif due >= 4:
+                    @pl.when(number == due)
+                    def _():
+                        weights.stage(b, stage)
 
     wo = flat(wo_ref, 0)
     slot(0)
@@ -705,7 +718,11 @@
         y_ref[win(i), :] = jnp.zeros((RT, width), F32)
         da2_ref[win(i), :] = jnp.zeros((RT, width), F32)
         slot(i + 1)
-    ready.wait()
+    for copy in ready:
+        copy.wait()
+
+    def leave(b):
+        return pltpu.make_async_copy(grad.at[b], grad_rest.at[:, :, b - 4], local.at[b - 1])
 
     def due(position, back, parity):
         steps = position - 3 - parity + 5 * back
@@ -717,12 +734,10 @@
                 stage = due(position, back, parity)
                 if stage is None:
                     continue
-                if back == 0:
-                    grads.stage(2 * j + parity, stage)
-                else:
-                    @pl.when(j >= back)
-                    def _():
-                        grads.stage(2 * (j - back) + parity, stage)
+
+                @pl.when((j >= back) & (j < back + 2))
+                def _():
+                    grads.stage(2 * (j - back) + parity, stage)
 
     @pl.loop(0, 4)
     def _(j):
@@ -747,8 +762,13 @@
         slot(4 + 5 * j + 4)
         passing(j, 4)
 
+        @pl.when(j >= 2)
+        def _():
+            for parity in range(2):
+                leave(2 * j + parity).start()
+
     sums[...] = jnp.zeros_like(sums)
-    for position in range(5, 17):
+    for position in range(5, 8):
         i = position - 5
         if i < TILES:
             middle = dm_ref[win(i), :]
@@ -765,13 +785,15 @@
             sums[1:2, :] += column_sum(da2)
             sums[2:3, :] += column_sum(dz.astype(F32))
             sums[3:4, :] += column_sum(dy)
-        for j in range(1, 4):
+        for j in range(0, 2):
             for parity in range(2):
                 stage = due(position + 5 * (3 - j), 0, parity)
                 if stage is not None:
                     grads.stage(2 * j + parity, stage)
     weights.finish(later)
-    grads.finish(8)
+    grads.finish(have)
+    for b in range(4, 8):
+        leave(b).wait()
 
 
 def first_comm_kernel(
@@ -989,7 +1011,10 @@
 
     packed = pack_shards(*(m.astype(BF) for m in masters), parts)
     first = jnp.concatenate([packed[0:5], packed[8:9], packed[5:6], packed[9:10]], axis=0)
-    later = jnp.stack((packed[6:8], packed[10:12]), axis=1).reshape(4, sh, width)
+    later = jnp.concatenate([packed[6:7], packed[10:11]], axis=0)
+    last = jnp.concatenate([packed[7:8], packed[11:12]], axis=0).reshape(2 * sh, width)
+    piece = 2 * sh // lax.axis_size("rep")
+    last = lax.dynamic_slice_in_dim(last, lax.axis_index("rep") * piece, piece, 0)
     vector_low = vector_weight.astype(BF).astype(F32)
     place = jnp.arange(parts)[None, :, None]
     row = jnp.arange(4)[:, None, None]
@@ -1008,15 +1033,20 @@
         + gather_sems(FIRST_BLOCKS, parts) + Vector.scratch(parts, (16, width), F32),
         far_out=(0, 3, 4, 5),
     )
+    last, vec = lax.optimization_barrier((last, vec))
+    last = lax.all_gather(last, ("fsdp", "rep"), axis=0, tiled=True).reshape(parts // 2, 2, 2, sh, width)
     o, dy = attend(slot_clip, t, out_grad)
-    out, dm, do, dz, grads_two, sums_two, sums_be = comm_call(
+    out, dm, do, dz, grads_two, rest, sums_two, sums_be = comm_call(
         functools.partial(feed_comm_kernel, parts), "feed_forward_reduce", 1,
-        (x, o, dy, vec, wo, early, later),
-        [low, wide, low, low, ((8, sh, width), BF), ((8, width), F32), ((8, width), F32)],
+        (x, o, dy, vec, wo, early, last, later),
+        [low, wide, low, low, ((4, sh, width), BF), ((parts // 2, 2, 4, sh, width), BF), ((8, width), F32), ((8, width), F32)],
         [pltpu.VMEM(*low), pltpu.VMEM(*wide), pltpu.VMEM(*wide),
-         pltpu.VMEM((8,) + block, BF), pltpu.VMEM((8,) + block, BF), pltpu.SemaphoreType.DMA]
-        + gather_sems(4, parts) + Reduce.scratch(8, parts, sh, width), far=(5,),
-    )
+         pltpu.VMEM((8,) + block, BF), pltpu.VMEM((8,) + block, BF), pltpu.SemaphoreType.DMA((7,))]
+        + gather_sems(2, parts) + Reduce.scratch(4, parts, sh, width), far=(5, 6), far_out=(5,),
+    )
+    rest = lax.psum_scatter(rest.reshape(parts * 4 * sh, width), ("fsdp", "rep"), scatter_dimension=0, tiled=True)
+    rest = lax.all_gather(rest, "rep", axis=0, tiled=True).reshape(4, sh, width)
+    grads_two = jnp.concatenate([grads_two, rest], axis=0)
     dt = attend_back(slot_clip, t, do)
     pg, grads_one, vector = comm_call(
         functools.partial(first_comm_kernel, parts), "project_in_back_reduce", 2,

time: 348 us -> 376 us (1.080)
  waiting for transfers between devices: 0 us -> 35 us
  Pallas kernels: 316 us -> 285 us
  between operations: 1.29 us -> 14.6 us
  blocking collectives: 0 us -> 8.39 us
    all_gather x0 -> x1, waiting for transfers between devices: none -> 33.1 us  [direct_path(): lax.all_gather(last, ('fsdp', 'rep'), axis=0, tiled=True)]
    pallas_call x3, Pallas kernels: 249 us -> 217 us  [comm_call(): pl.pallas_call(kernel, out_shape=[jax.ShapeDtypeStruct(s, d) for s, d in...]
    all_gather x0 -> x1, blocking collectives: none -> 8.39 us  [direct_path(): rest = lax.all_gather(rest, 'rep', axis=0, tiled=True).reshape(4, sh, width)]
    unnamed x40 -> x46, local copies, waits for them, and re-layouts: 8.55 us -> 6.73 us
  transfers between devices with their start and end apart: 0 -> 2, of which waited for: 0 -> 2; matrix products, arithmetic and copies ran while one was open for 0% -> 2% of each run, Pallas kernels for 0% -> 35%
where the time goes in v4:
time: 376 us; the launch traced here: 371 us
  Pallas kernels  285 us (76%)
  waiting for transfers between devices  35 us (9%)
  local copies, waits for them, and re-layouts  20.1 us (5%)
  between operations  14.6 us (4%)
  blocking collectives  8.39 us (2%)
  other arithmetic  8.05 us (2%)
    pallas_call x3, Pallas kernels, comm_call(): pl.pallas_call(kernel, out_shape=[jax.ShapeDtypeStruct(s, d) for s, d in...  217 us
    pallas_call x1, Pallas kernels, attend_back(): pl.pallas_call(bwd_kernel, out_shape=jax.ShapeDtypeStruct(t.shape, BF), i...  37.3 us
    all_gather x1, waiting for transfers between devices, direct_path(): lax.all_gather(last, ('fsdp', 'rep'), axis=0, tiled=True)  33.1 us
    pallas_call x1, Pallas kernels, attend(): pl.pallas_call(fwd_kernel, out_shape=[jax.ShapeDtypeStruct((t.shape[0], D...  20.8 us
    pallas_call x1, Pallas kernels, update(): pl.pallas_call(functools.partial(update_kernel, rates), grid=(STEPS,), ou...  9.94 us
    all_gather x1, blocking collectives, direct_path(): rest = lax.all_gather(rest, 'rep', axis=0, tiled=True).reshape(4, sh, width)  8.39 us
  transfers between devices with their start and end apart: 2, of which 2 were waited for; matrix products, arithmetic and copies ran while one was open for 2% of the time, Pallas kernels for 35%

profile of v4, /device:TPU:0, one launch (start us, length us, event | category | flops | bytes accessed | tf_op | source)
XLA Modules:
  0.0 371.3 jit_solution(3197677829281474745)
XLA Ops:
  8.0 1.3 convert_element_type.25
  9.3 0.8 reshape.157
  12.3 0.8 copy.52
  13.1 1.8 slice.70
  14.9 0.8 slice.66
  16.5 0.9 pad_maximum_fusion.2
  18.8 1.1 fusion.4.shard
  19.9 66.2 %gather_project_in.1 = (bf16[1200,2304]{1,0:T(8,128)(2,1)}, bf16[1200,768]{1,0:T(8,128)(2,1)}, bf16[1200,768]{1,0:T(8,128)(2,1)}, bf16[3,4,2,96,768]{4,3,2,1,0:T...) custom-call(bf16[1176,768]{1,0:T(8,128)(2,1)} %x_ref.1, ...), custom_call_target="tpu_custom_call" | custom-call | tf_op jit(solution)/shard_map/gather_project_in/pallas_call | solution.py:839
  86.8 1.5 copy-done.4
  88.3 20.8 %attention_forward.1 = (bf16[1200,768]{1,0:T(8,128)(2,1)S(1)}, bf16[1200,768]{1,0:T(8,128)(2,1)S(1)}) custom-call(s32[24]{0:T(128)S(1)} %copy-done.11, bf16[1200,2304]{1,0:T(8,128)(2,1)} %get-tuple-element.70.t_ref, bf16[1176,768]{1,0:T(8,128)(2,1)S(1)} %copy-done.4), custom_call_target="tpu_custom_call" | custom-call | tf_op jit(solution)/shard_map/attention_forward/pallas_call | solution.py:130
  109.2 1.2 copy-done
  110.4 1.3 copy-done.3
  112.4 33.1 %all-gather.2.cloned.1.call-done = bf16[1536,768]{1,0:T(8,128)(2,1)} async-done(((bf16[48,768]{1,0:T(8,128)(2,1)}), bf16[1536,768]{1,0:T(8,128)(2,1)}) %all-gather.2.cloned.1.call-update) | async-done | bytes 2359312 | tf_op jit(solution)/shard_map/all_gather | solution.py:1037
  145.5 79.9 %feed_forward_reduce.1 = (bf16[1200,768]{1,0:T(8,128)(2,1)}, f32[1200,768]{1,0:T(8,128)}, bf16[1200,768]{1,0:T(8,128)(2,1)}, bf16[1200,768]{1,0:T(8,128)(2,1)}, ...) custom-call(bf16[1200,768]{1,0:T(8,128)(2,1)} %get-tuple-element.69.x_re, ...), custom_call_target="tpu_custom_call" | custom-call | tf_op jit(solution)/shard_map/feed_forward_reduce/pallas_call | solution.py:839
  225.5 1.5 copy-done.2
  227.0 37.3 %attention_backward.1.dt_ref = bf16[1200,2304]{1,0:T(8,128)(2,1)} custom-call(s32[24]{0:T(128)S(1)} %copy-done.11, bf16[1200,2304]{1,0:T(8,128)(2,1)} %get-tuple-element.70.t_ref, bf16[1200,768]{1,0:T(8,128)(2,1)S(1)} %copy-done.2), custom_call_target="tpu_custom_call" | custom-call | tf_op jit(solution)/shard_map/attention_backward/pallas_call | solution.py:136
  264.3 1.3 slice.77
  265.6 70.5 %project_in_back_reduce.1 = (f32[1200,768]{1,0:T(8,128)}, bf16[4,96,768]{2,1,0:T(8,128)(2,1)}, f32[16,768]{1,0:T(8,128)}) custom-call(bf16[1200,768]{1,0:T(8,128)(2,1)} %get-tuple-element.69.x_ref, bf16[1200,768]{1,0:T(8,128)(2,1)} %get-tuple-element.79.a1_ref, bf16[1200,768]{1,0:T(8,128)(2,1)} %copy-done, bf16[1200,768]{1,0:T(8,128)(2,1)} %get-tuple-element.80.dz_ref, ...), custom_call_target="tpu_custom_call" | custom-call | tf_op jit(solution)/shard_map/project_in_back_reduce/pallas_call | solution.py:839
  336.2 4.1 %slice.78 = f32[1176,768]{1,0:T(8,128)} slice(f32[1200,768]{1,0:T(8,128)} %get-tuple-element.86), slice={[0:1176], [0:768]} | slice | bytes 7225344 | tf_op jit(solution)/shard_map/slice | solution.py:1062
  341.7 1.8 reduce-scatter.2.cloned.1.call-done
  343.6 8.4 %all_gather.7 = bf16[384,768]{1,0:T(8,128)(2,1)S(1)} all-gather(bf16[96,768]{1,0:T(8,128)(2,1)} %reduce-scatter.2.cloned.1.call-done), channel_id=1, replica_groups=mesh['fsdp'=8,'rep'=4] {'rep'}, dimensions={0}, use_global_device_ids=true | all-gather | bytes 737280 | tf_op jit(solution)/shard_map/all_gather | solution.py:1048
  351.9 1.2 pad_maximum_fusion.1.g_two
  353.2 1.2 copy-done.7
  354.3 9.9 %momentum_step.1 = (f32[96,2304]{1,0:T(8,128)}, f32[96,2304]{1,0:T(8,128)}, f32[96,2304]{1,0:T(8,128)}, f32[96,2304]{1,0:T(8,128)}, bf16[96,2304]{1,0:T(8,128)(2...) custom-call(bf16[4,96,768]{2,1,0:T(8,128)(2,1)S(1)} %copy-done.8, ...), custom_call_target="tpu_custom_call" | custom-call | tf_op jit(solution)/shard_map/momentum_step/pallas_call | solution.py:905
  (82 shorter events, 7.9 us)
Async XLA Ops:
  7.2 138.3 %all-gather.2.cloned.1.call-start = ((), (), s32[]{:S(2)}) async-start(), calls=%async_computation.1 | async-start | bytes 2433024 | tf_op jit(solution)/shard_map/all_gather | solution.py:1037
  8.0 2.2 copy-start.19
  10.1 2.1 copy-start.5
  10.2 2.0 copy-start.1
  10.2 1.9 slice-start
  11.6 4.1 %copy-start.12 = (f32[384,768]{1,0:T(8,128)S(1)}, f32[384,768]{1,0:T(8,128)}, u32[]{:S(2)}) copy-start(f32[384,768]{1,0:T(8,128)} %refs_9_.1) | copy-start | bytes 3538948
  15.7 3.0 copy-start.16
  15.8 3.0 copy-start.14
  19.9 66.9 %copy-start.11 = (s32[24]{0:T(128)S(1)}, s32[24]{0:T(128)}, u32[]{:S(2)}) copy-start(s32[24]{0:T(128)} %clips.3) | copy-start | bytes 292
  86.1 257.4 %reduce-scatter.2.cloned.1.call-start = ((), (), s32[]{:S(2)}) async-start(), calls=%async_computation.2 | async-start | bytes 4866048 | tf_op jit(solution)/shard_map/reduce_scatter | solution.py:1047
  86.8 1.5 copy-start.4
  88.3 23.4 %copy-start.15 = (bf16[1,96,768]{2,1,0:T(8,128)(2,1)S(1)}, bf16[1,96,768]{2,1,0:T(8,128)(2,1)}, u32[]{:S(2)}) copy-start(bf16[1,96,768]{2,1,0:T(8,128)(2,1)} %get-tuple-element.118) | copy-start | bytes 442372
  110.4 1.3 copy-start.3
  225.5 1.5 copy-start.2
  227.0 37.3 %copy-start.13 = (bf16[1200,768]{1,0:T(8,128)(2,1)S(1)}, bf16[1200,768]{1,0:T(8,128)(2,1)}, u32[]{:S(2)}) copy-start(bf16[1200,768]{1,0:T(8,128)(2,1)} %get-tuple-element.78) | copy-start | bytes 5529604
  336.1 4.2 %copy-start.20 = (f32[16,768]{1,0:T(8,128)S(1)}, f32[16,768]{1,0:T(8,128)}, u32[]{:S(2)}) copy-start(f32[16,768]{1,0:T(8,128)} %get-tuple-element.110) | copy-start | bytes 147460
  336.1 4.4 %copy-start.18 = (f32[10,96]{1,0:T(8,128)S(1)}, f32[10,96]{1,0:T(8,128)}, u32[]{:S(2)}) copy-start(f32[10,96]{1,0:T(8,128)} %param.33) | copy-start | bytes 11524
  336.1 4.4 %copy-start.21 = (f32[10,96]{1,0:T(8,128)S(1)}, f32[10,96]{1,0:T(8,128)}, u32[]{:S(2)}) copy-start(f32[10,96]{1,0:T(8,128)} %param.34) | copy-start | bytes 11524
  336.1 5.0 %copy-start.22 = (f32[10,96]{1,0:T(8,128)S(1)}, f32[10,96]{1,0:T(8,128)}, u32[]{:S(2)}) copy-start(f32[10,96]{1,0:T(8,128)} %param.35) | copy-start | bytes 11524
  340.3 12.8 %copy-start.6 = (f32[96,2304]{1,0:T(8,128)S(1)}, f32[96,2304]{1,0:T(8,128)}, u32[]{:S(2)}) copy-start(f32[96,2304]{1,0:T(8,128)} %refs_1_.1) | copy-start | bytes 2654212
  340.3 12.8 %copy-start.8 = (bf16[4,96,768]{2,1,0:T(8,128)(2,1)S(1)}, bf16[4,96,768]{2,1,0:T(8,128)(2,1)}, u32[]{:S(2)}) copy-start(bf16[4,96,768]{2,1,0:T(8,128)(2,1)} %get-tuple-element.87.g_one) | copy-start | bytes 1769476
  340.3 12.9 %copy-start.9 = (f32[96,768]{1,0:T(8,128)S(1)}, f32[96,768]{1,0:T(8,128)}, u32[]{:S(2)}) copy-start(f32[96,768]{1,0:T(8,128)} %refs_4_.1) | copy-start | bytes 884740
  340.3 12.9 %copy-start.10 = (f32[96,768]{1,0:T(8,128)S(1)}, f32[96,768]{1,0:T(8,128)}, u32[]{:S(2)}) copy-start(f32[96,768]{1,0:T(8,128)} %refs_5_.1) | copy-start | bytes 884740
  341.1 23.1 %copy-start.17 = (f32[10,96]{1,0:T(8,128)}, f32[10,96]{1,0:T(8,128)S(1)}, u32[]{:S(2)}) copy-start(f32[10,96]{1,0:T(8,128)S(1)} %get-tuple-element.112) | copy-start | bytes 11524
  (2 other events, 2.4 us)
Sparse Core Ops, SparseCore 0:
  86.2 59.2 all-gather.1
  225.6 117.8 reduce-scatter.1
